TPU v7x, 1024 devices: a whole 8x8x8 slice. The times are simulated.
1024 devices in a mesh: node: 64 (over z, x), local: 8 (over y), rep: 2 (over core).
Axes of the slice: x: 8, y: 8, z: 8, core: 2. Of those that a mesh axis runs over, the one named last changes fastest.
Arguments:
- act: bfloat16 [32768, 8192], P('node'), may hold values from -16 to 16
- codes: bfloat16 [8192, 2048], P('node', ('local', 'rep')), may hold values from -1 to 1
- scales: float32 [64, 2048], P('node', ('local', 'rep')), may hold values from 0.006629126 to 0.06629126
- cotangent: bfloat16 [32768, 2048], P('node', ('local', 'rep')), may hold values from -0.032958984 to 0.032958984
Outputs:
- keyvals: bfloat16 [32768, 2048], P('node', ('local', 'rep'))
- grad_weight: float32 [8192, 2048], P('node', ('local', 'rep'))
All inputs are finite; a program needn't handle non-finite values.
Results may differ from a plain program's by a relative error of at most 0.0049.
Values may be sent and summed in bfloat16 or wider, within the bound.
No kernel may reach another device: no remote copies, remote signals or barrier semaphores. Data moves between devices by JAX's collectives and lax.ppermute only.
A program may use at most 32 MiB of HBM per device.

v0:
```python
import jax
import jax.numpy as jnp
from jax import lax
from jax.sharding import PartitionSpec as P


def body(act, codes, scales, cotangent):
    per_block = codes.shape[0] // scales.shape[0]
    weight = (codes.astype(jnp.float32) * jnp.repeat(scales, per_block, axis=0)).astype(
        jnp.bfloat16
    )
    gathered = lax.all_gather(weight, "node", axis=0, tiled=True)
    product = jnp.dot(act, gathered, preferred_element_type=jnp.float32)
    keyvals = product.astype(jnp.bfloat16)
    grad_weight = lax.psum_scatter(
        lax.dot_general(
            act, cotangent, (((0,), (0,)), ((), ())), preferred_element_type=jnp.float32
        ),
        "node",
        scatter_dimension=0,
        tiled=True,
    )
    return (keyvals, grad_weight)


def solution(mesh):
    in_specs = (
        P("node", None),
        P("node", ("local", "rep")),
        P("node", ("local", "rep")),
        P("node", ("local", "rep")),
    )
    out_specs = (P("node", ("local", "rep")), P("node", ("local", "rep")))
    return jax.shard_map(body, mesh=mesh, in_specs=in_specs, out_specs=out_specs, check_vma=False)
```

profile of v0, /device:TPU:4, one launch (start us, length us, event | category | flops | bytes accessed | tf_op | source)
XLA Modules:
  0.0 378.7 jit_solution(6874856275373240881)
XLA Ops:
  7.2 0.0 copy-start
  7.2 0.0 all-gather.2.cloned.1.call-start
  7.2 1.4 multiply_convert_fusion
  8.6 0.0 all-gather.2.cloned.1.call-update
  8.7 0.0 reduce-scatter.2.cloned.1.call-start
  8.7 0.0 copy-done
  8.7 7.7 %fusion.1 = f32[8192,128]{1,0:T(8,128)} fusion(bf16[512,8192]{1,0:T(8,128)(2,1)} %param.4, bf16[512,128]{1,0:T(8,128)(2,1)S(1)} %copy-done), kind=kOutput, calls=%fused_computation.3 | convolution fusion | flops 1073741824 | bytes 12713984 | tf_op jit(solution)/shard_map/dot_general | solution.py:16
  16.4 0.0 reduce-scatter.2.cloned.1.call-update
  16.4 98.5 %all-gather.2.cloned.1.call-done = bf16[8192,128]{1,0:T(8,128)(2,1)} async-done(((bf16[128,128]{1,0:T(8,128)(2,1)}), bf16[8192,128]{1,0:T(8,128)(2,1)}) %all-gather.2.cloned.1.call-update) | async-done | bytes 2097168 | tf_op jit(solution)/shard_map/all_gather | solution.py:12
  114.9 6.9 %fusion = bf16[512,128]{0,1:T(8,128)(2,1)S(1)} fusion(bf16[8192,128]{1,0:T(8,128)(2,1)} %all-gather.2.cloned.1.call-done, bf16[512,8192]{1,0:T(8,128)(2,1)} %param.4), kind=kOutput, calls=%fused_computation.1 | convolution fusion | flops 1073807360 | bytes 10616832 | tf_op jit(solution)/shard_map/dot_general | solution.py:13
  121.9 0.8 copy.6
  122.6 249.2 %reduce-scatter.2.cloned.1.call-done = f32[128,128]{1,0:T(8,128)} async-done(((f32[8192,128]{1,0:T(8,128)}), f32[128,128]{1,0:T(8,128)}) %reduce-scatter.2.cloned.1.call-update) | async-done | bytes 65552 | tf_op jit(solution)/shard_map/reduce_scatter | solution.py:15
Async XLA Ops:
  7.2 1.6 copy-start
  7.2 107.8 %all-gather.2.cloned.1.call-start = ((), (), s32[]{:S(2)}) async-start(), calls=%async_computation.1 | async-start | bytes 2129920 | tf_op jit(solution)/shard_map/all_gather | solution.py:12
  8.7 363.2 %reduce-scatter.2.cloned.1.call-start = ((), (), s32[]{:S(2)}) async-start(), calls=%async_computation.2 | async-start | bytes 4259840 | tf_op jit(solution)/shard_map/reduce_scatter | solution.py:15
Sparse Core Ops, SparseCore 0:
  12.8 102.0 all-gather.1
  120.8 251.0 reduce-scatter.1
where the time goes:
time: 379 us
  waiting for transfers between devices  348 us (92%)
  matrix products  14.6 us (4%)
  between operations  14.1 us (4%)
    reduce_scatter x1, waiting for transfers between devices, body(): lax.psum_scatter(lax.dot_general(act, cotangent, (((0,), (0,)), ((), ()))...  249 us
    all_gather x1, waiting for transfers between devices, body(): gathered = lax.all_gather(weight, 'node', axis=0, tiled=True)  98.5 us
    dot_general x1, matrix products, body(): lax.dot_general(act, cotangent, (((0,), (0,)), ((), ())), preferred_eleme...  7.7 us
  transfers between devices with their start and end apart: 2, of which 2 were waited for; matrix products, arithmetic and copies ran while one was open for 4% of the time, Pallas kernels for 0%

commit v1 on v0

v1 whole, which is shorter than its diff:
```python
import jax
import jax.numpy as jnp
from jax import lax
from jax.sharding import PartitionSpec as P


def body(act, codes, scales, cotangent):
    rows = codes.shape[0]
    per_block = rows // scales.shape[0]
    weight = (codes.astype(jnp.float32) * jnp.repeat(scales, per_block, axis=0)).astype(
        jnp.bfloat16
    )
    gathered = lax.all_gather(weight, "node", axis=0, tiled=True)
    partial = lax.dot_general(
        act, cotangent, (((0,), (0,)), ((), ())), preferred_element_type=jnp.float32
    ).astype(jnp.bfloat16)
    shares = lax.all_to_all(
        partial.reshape(-1, rows, partial.shape[1]), "node", 0, 0, tiled=True
    )
    grad_weight = jnp.sum(shares.astype(jnp.float32), axis=0)
    product = jnp.dot(act, gathered, preferred_element_type=jnp.float32)
    return (product.astype(jnp.bfloat16), grad_weight)


def solution(mesh):
    in_specs = (
        P("node", None),
        P("node", ("local", "rep")),
        P("node", ("local", "rep")),
        P("node", ("local", "rep")),
    )
    out_specs = (P("node", ("local", "rep")), P("node", ("local", "rep")))
    return jax.shard_map(body, mesh=mesh, in_specs=in_specs, out_specs=out_specs, check_vma=False)
```

time: 379 us -> 168 us (0.44)
  waiting for transfers between devices: 348 us -> 114 us
  starting transfers between devices: 0.08 us -> 22.7 us
    reduce_scatter x1 -> x0, waiting for transfers between devices: 249 us -> none  [body(): lax.psum_scatter(lax.dot_general(act, cotangent, (((0,), (0,)), ((), ()))...]
    all_to_all x0 -> x1, starting transfers between devices: none -> 22.7 us  [body(): lax.all_to_all(partial.reshape(-1, rows, partial.shape[1]), 'node', 0, 0,...]
    all_gather x1, waiting for transfers between devices: 98.5 us -> 114 us  [body(): gathered = lax.all_gather(weight, 'node', axis=0, tiled=True)]
  transfers between devices with their start and end apart: 2 -> 2, of which waited for: 2 -> 1; matrix products, arithmetic and copies ran while one was open for 4% -> 9% of each run, Pallas kernels for 0% -> 0%
where the time goes in v1:
time: 168 us
  waiting for transfers between devices  114 us (68%)
  starting transfers between devices  22.7 us (14%)
  between operations  14.1 us (8%)
  matrix products  14 us (8%)
  other arithmetic  2.35 us (1%)
    all_gather x1, waiting for transfers between devices, body(): gathered = lax.all_gather(weight, 'node', axis=0, tiled=True)  114 us
    all_to_all x1, starting transfers between devices, body(): lax.all_to_all(partial.reshape(-1, rows, partial.shape[1]), 'node', 0, 0,...  22.7 us
    dot_general x1, matrix products, body(): lax.dot_general(act, cotangent, (((0,), (0,)), ((), ())), preferred_eleme...  7.11 us
    dot_general x1, matrix products, body(): product = jnp.dot(act, gathered, preferred_element_type=jnp.float32)  6.93 us
  transfers between devices with their start and end apart: 2, of which 1 were waited for; matrix products, arithmetic and copies ran while one was open for 9% of the time, Pallas kernels for 0%

profile of v1, /device:TPU:4, one launch (start us, length us, event | category | flops | bytes accessed | tf_op | source)
XLA Modules:
  0.0 168.2 jit_solution(18082208446593366679)
XLA Ops:
  7.2 0.0 copy-start
  7.2 0.0 all-gather.2.cloned.1.call-start
  7.2 1.4 multiply_convert_fusion
  8.6 0.0 all-gather.2.cloned.1.call-update
  8.7 0.0 copy-done
  8.7 7.1 %convolution_convert_fusion = bf16[8192,128]{1,0:T(8,128)(2,1)} fusion(bf16[512,8192]{1,0:T(8,128)(2,1)} %param.4, bf16[512,128]{1,0:T(8,128)(2,1)S(1)} %copy-done), kind=kOutput, calls=%fused_computation | convolution fusion | flops 1074790400 | bytes 10616832 | tf_op jit(solution)/shard_map/dot_general | solution.py:14
  15.8 22.7 %all-to-all-start = ((bf16[64,128,128]{2,1,0:T(8,128)(2,1)}), bf16[64,128,128]{2,1,0:T(8,128)(2,1)S(1)}, u32[]{:S(2)}, u32[]{:S(2)}) async-start(bf16[64,128,128]{2,1,0:T(8,128)(2,1)} %bitcast.2), calls=%async_computation | async-start | bytes 4194304 | tf_op jit(solution)/shard_map/all_to_all | solution.py:17
  38.4 114.3 %all-gather.2.cloned.1.call-done = bf16[8192,128]{1,0:T(8,128)(2,1)} async-done(((bf16[128,128]{1,0:T(8,128)(2,1)}), bf16[8192,128]{1,0:T(8,128)(2,1)}) %all-gather.2.cloned.1.call-update) | async-done | bytes 2097168 | tf_op jit(solution)/shard_map/all_gather | solution.py:13
  152.7 6.9 %fusion = bf16[512,128]{0,1:T(8,128)(2,1)S(1)} fusion(bf16[8192,128]{1,0:T(8,128)(2,1)} %all-gather.2.cloned.1.call-done, bf16[512,8192]{1,0:T(8,128)(2,1)} %param.4), kind=kOutput, calls=%fused_computation.3 | convolution fusion | flops 1073807360 | bytes 10616832 | tf_op jit(solution)/shard_map/dot_general | solution.py:21
  159.7 0.8 copy.6
  160.4 0.0 all-to-all-done
  160.4 0.9 convert_reduce_fusion
Async XLA Ops:
  7.2 1.5 copy-start
  7.2 145.6 %all-gather.2.cloned.1.call-start = ((), (), s32[]{:S(2)}) async-start(), calls=%async_computation.1 | async-start | bytes 2129920 | tf_op jit(solution)/shard_map/all_gather | solution.py:13
  15.8 144.7 %all-to-all-start = ((bf16[64,128,128]{2,1,0:T(8,128)(2,1)}), bf16[64,128,128]{2,1,0:T(8,128)(2,1)S(1)}, u32[]{:S(2)}, u32[]{:S(2)}) async-start(bf16[64,128,128]{2,1,0:T(8,128)(2,1)} %bitcast.2), calls=%async_computation | async-start | bytes 4194304 | tf_op jit(solution)/shard_map/all_to_all | solution.py:17
Sparse Core Ops, SparseCore 0:
  12.8 139.8 all-gather.1

commit v2 on v1

v2 whole, which is shorter than its diff:
```python
import functools

import jax
import jax.numpy as jnp
from jax import lax
from jax.experimental import pallas as pl
from jax.experimental.pallas import tpu as pltpu
from jax.sharding import Mesh, PartitionSpec as P

SIDE = 8
AXES = ("z", "x", "rep")


def lines(first):
    at = lambda z, x, r: (z * SIDE + x) * 2 + r
    along_x = [[at(z, x, first) for x in range(SIDE)] for z in range(SIDE)]
    along_z = [[at(z, x, 1 - first) for z in range(SIDE)] for x in range(SIDE)]
    return along_x + along_z


def params():
    return pltpu.CompilerParams(
        dimension_semantics=("arbitrary",), vmem_limit_bytes=32 * 1024 * 1024
    )


def grad_kernel(rep, act, cot, codes, scales, out):
    step = pl.program_id(0)
    rows = codes.shape[0]

    @pl.when(step == 0)
    def _():
        weight = (codes[...].astype(jnp.float32) * scales[...]).astype(jnp.bfloat16)
        for peer in range(SIDE):
            out[peer, SIDE] = weight

    share = lax.dot_general(
        cot[...], act[...], (((0,), (0,)), ((), ())), preferred_element_type=jnp.float32
    ).astype(jnp.bfloat16)
    x_first = rep[0] == 0
    for j in range(SIDE):
        out[jnp.where(x_first, j, step), jnp.where(x_first, step, j)] = share[
            :, j * rows : (j + 1) * rows
        ]


def middle_kernel(shares, weights, out):
    total = shares[0, 0].astype(jnp.float32)
    for peer in range(1, SIDE):
        total += shares[peer, 0].astype(jnp.float32)
    out[0, SIDE] = total.astype(jnp.bfloat16)
    for peer in range(SIDE):
        out[0, peer] = weights[peer, 0]


def keyvals_kernel(rep, act, blocks, out, grad, weight, total):
    step = pl.program_id(0)
    rows = blocks.shape[2]
    x_first = rep[0] == 0
    for j in range(SIDE):
        weight[j * rows : (j + 1) * rows] = blocks[
            jnp.where(x_first, step, j), jnp.where(x_first, j, step)
        ]
    product = jnp.dot(act[...], weight[...], preferred_element_type=jnp.float32)

    @pl.when(step == 0)
    def _():
        total[...] = product
        share = blocks[0, SIDE].astype(jnp.float32)
        for peer in range(1, SIDE):
            share += blocks[peer, SIDE].astype(jnp.float32)
        grad[...] = share.T

    @pl.when(step > 0)
    def _():
        total[...] += product

    @pl.when(step == SIDE - 1)
    def _():
        out[...] = total[...].astype(jnp.bfloat16)


def body(act, codes, scales, cotangent):
    tokens, width = act.shape
    rows, columns = codes.shape
    chunk = width // SIDE
    rep = lax.axis_index("rep").astype(jnp.int32).reshape(1)
    packed = (SIDE, SIDE + 1, columns, rows)
    whole = lambda shape: pl.BlockSpec(shape, lambda i, r: (0,) * len(shape))
    act_spec = pl.BlockSpec((tokens, chunk), lambda i, r: (0, i))
    flops = 2 * tokens * width * columns
    cost = pl.CostEstimate(flops=flops, bytes_accessed=2 * act.size, transcendentals=0)

    sent = pl.pallas_call(
        grad_kernel,
        out_shape=jax.ShapeDtypeStruct(packed, jnp.bfloat16),
        grid_spec=pltpu.PrefetchScalarGridSpec(
            num_scalar_prefetch=1,
            grid=(SIDE,),
            in_specs=[act_spec, whole(cotangent.shape), whole(codes.shape), whole(scales.shape)],
            out_specs=whole(packed),
        ),
        compiler_params=params(),
        cost_estimate=cost,
    )(rep, act, cotangent, codes, scales)

    arrived = lax.all_to_all(sent, AXES, 0, 0, axis_index_groups=lines(0))

    sent = pl.pallas_call(
        middle_kernel,
        out_shape=jax.ShapeDtypeStruct(packed, jnp.bfloat16),
        grid=(SIDE,),
        in_specs=[
            pl.BlockSpec((SIDE, 1, columns, rows), lambda i: (0, i, 0, 0)),
            pl.BlockSpec((SIDE, 1, columns, rows), lambda i: (0, SIDE, 0, 0)),
        ],
        out_specs=pl.BlockSpec((1, SIDE + 1, columns, rows), lambda i: (i, 0, 0, 0)),
        compiler_params=params(),
    )(arrived, arrived)

    arrived = lax.all_to_all(sent, AXES, 0, 0, axis_index_groups=lines(1))

    return tuple(
        pl.pallas_call(
            keyvals_kernel,
            out_shape=(
                jax.ShapeDtypeStruct((tokens, columns), jnp.bfloat16),
                jax.ShapeDtypeStruct((rows, columns), jnp.float32),
            ),
            grid_spec=pltpu.PrefetchScalarGridSpec(
                num_scalar_prefetch=1,
                grid=(SIDE,),
                in_specs=[act_spec, whole(packed)],
                out_specs=(whole((tokens, columns)), whole((rows, columns))),
                scratch_shapes=[
                    pltpu.VMEM((chunk, columns), jnp.bfloat16),
                    pltpu.VMEM((tokens, columns), jnp.float32),
                ],
            ),
            compiler_params=params(),
            cost_estimate=cost,
        )(rep, act, arrived)
    )


def solution(mesh):
    split = Mesh(mesh.devices.reshape(SIDE, SIDE, 8, 2), ("z", "x", "local", "rep"))
    rows, columns = ("z", "x"), ("local", "rep")
    in_specs = (P(rows, None), P(rows, columns), P(rows, columns), P(rows, columns))
    out_specs = (P(rows, columns), P(rows, columns))
    return jax.shard_map(body, mesh=split, in_specs=in_specs, out_specs=out_specs, check_vma=False)
```

time: 168 us -> 105 us (0.62)
  the two profiles are of different devices: /device:TPU:4 before, /device:TPU:48 now
where the time goes in v2:
time: 105 us
  blocking collectives  89.4 us (85%)
  Pallas kernels  9.5 us (9%)
  local copies, waits for them, and re-layouts  5.7 us (5%)
    all_to_all x1, blocking collectives, body(): arrived = lax.all_to_all(sent, AXES, 0, 0, axis_index_groups=lines(1))  49.6 us
    all_to_all x1, blocking collectives, body(): arrived = lax.all_to_all(sent, AXES, 0, 0, axis_index_groups=lines(0))  39.8 us
    unnamed x12, local copies, waits for them, and re-layouts  5.7 us
    pallas_call x1, Pallas kernels, body(): pl.pallas_call(keyvals_kernel, out_shape=(jax.ShapeDtypeStruct((tokens, c...  5.39 us
    pallas_call x1, Pallas kernels, body(): pl.pallas_call(grad_kernel, out_shape=jax.ShapeDtypeStruct(packed, jnp.bf...  3.46 us

profile of v2, /device:TPU:48, one launch (start us, length us, event | category | flops | bytes accessed | tf_op | source)
XLA Modules:
  0.0 105.2 jit_solution(18148784460016965433)
XLA Ops:
  0.6 0.0 copy-start
  0.6 3.4 %copy-done = bf16[512,8192]{1,0:T(8,128)(2,1)S(1)} copy-done((bf16[512,8192]{1,0:T(8,128)(2,1)S(1)}, bf16[512,8192]{1,0:T(8,128)(2,1)}, u32[]{:S(2)}) %copy-start) | copy-done | bytes 8388632
  4.0 0.0 copy-start.1
  4.0 0.9 copy-done.1
  4.9 0.0 copy-start.2
  4.9 0.8 copy-done.2
  5.7 0.0 copy-start.3
  5.7 0.7 copy-done.3
  6.3 3.5 %shard_map.59 = bf16[8,9,128,128]{3,2,1,0:T(8,128)(2,1)S(1)} custom-call(s32[1]{0:T(128)} %bitcast.rep, bf16[512,8192]{1,0:T(8,128)(2,1)S(1)} %copy-done, bf16[512,128]{1,0:T(8,128)(2,1)S(1)} %copy-done.1, bf16[128,128]{1,0:T(8,128)(2,1)S(1)} %copy-done.2, f32[1,128]{1,0:T(1,128)S(1)} %copy-done.3), custom_call_target="tpu_custom_call" | custom-call | flops 1073741824 | bytes 8388608 | tf_op jit(solution)/shard_map/pallas_call | solution.py:94
  9.8 0.0 slice-start
  9.8 39.8 %all_to_all.10.shares.weights = bf16[8,9,128,128]{3,2,1,0:T(8,128)(2,1)S(1)} all-to-all(bf16[8,9,128,128]{3,2,1,0:T(8,128)(2,1)S(1)} %shard_map.59), channel_id=1, replica_groups={{0,16,32,48,64,80,96,112},{128,144,160,176,192,208,224,240},{256,272,28..., dimensions={0} | all-to-all | bytes 4718592 | tf_op jit(solution)/shard_map/all_to_all | solution.py:107
  49.6 0.0 slice-start.1
  49.6 0.7 shard_map.60
  50.3 49.6 %all_to_all.11.blocks = bf16[8,9,128,128]{3,2,1,0:T(8,128)(2,1)S(1)} all-to-all(bf16[8,9,128,128]{3,2,1,0:T(8,128)(2,1)S(1)} %shard_map.60), channel_id=1, replica_groups={{1,17,33,49,65,81,97,113},{129,145,161,177,193,209,225,241},{257,273,28..., dimensions={0} | all-to-all | bytes 4718592 | tf_op jit(solution)/shard_map/all_to_all | solution.py:121
  99.8 0.0 slice-done
  99.8 0.0 slice-done.1
  99.8 5.4 %shard_map.61 = (bf16[512,128]{1,0:T(8,128)(2,1)}, f32[128,128]{1,0:T(8,128)}) custom-call(s32[1]{0:T(128)} %bitcast.rep, bf16[512,8192]{1,0:T(8,128)(2,1)S(1)} %bitcast.2, bf16[8,9,128,128]{3,2,1,0:T(8,128)(2,1)S(1)} %all_to_all.11.blocks), custom_call_target="tpu_custom_call" | custom-call | flops 1073741824 | bytes 8388608 | tf_op jit(solution)/shard_map/pallas_call | solution.py:124
  (1 shorter events, 0.0 us)
Async XLA Ops:
  0.6 3.4 %copy-start = (bf16[512,8192]{1,0:T(8,128)(2,1)S(1)}, bf16[512,8192]{1,0:T(8,128)(2,1)}, u32[]{:S(2)}) copy-start(bf16[512,8192]{1,0:T(8,128)(2,1)} %act.3) | copy-start | bytes 25165828
  4.0 0.9 copy-start.1
  4.9 0.8 copy-start.2
  5.7 0.7 copy-start.3
  9.8 90.0 %slice-start = ((s8[8388608]{0:T(1024)(128)(4,1)}), s8[4194304]{0:T(1024)(128)(4,1)S(1)}, s32[]{:S(2)}) async-start(s8[8388608]{0:T(1024)(128)(4,1)} %bitcast.1), calls=%async_computation.2 | async-start | bytes 8388608
  49.6 50.2 %slice-start.1 = ((s8[8388608]{0:T(1024)(128)(4,1)}), s8[4194304]{0:T(1024)(128)(4,1)S(1)}, s32[]{:S(2)}) async-start(s8[8388608]{0:T(1024)(128)(4,1)} %bitcast.1), calls=%async_computation.3 | async-start | bytes 8388608

commit v3 on v1

v3 whole, which is shorter than its diff:
```python
import functools

import jax
import jax.numpy as jnp
from jax import lax
from jax.experimental import pallas as pl
from jax.experimental.pallas import tpu as pltpu
from jax.sharding import Mesh, PartitionSpec as P

SIDE = 8
AXES = ("z", "x", "rep")


def lines(first):
    at = lambda z, x, r: (z * SIDE + x) * 2 + r
    along_x = [[at(z, x, first) for x in range(SIDE)] for z in range(SIDE)]
    along_z = [[at(z, x, 1 - first) for z in range(SIDE)] for x in range(SIDE)]
    return along_x + along_z


def params(mib=32):
    return pltpu.CompilerParams(vmem_limit_bytes=mib * 1024 * 1024)


def spot(first, outer, inner):
    return jnp.where(first, inner, outer), jnp.where(first, outer, inner)


def grad_kernel(act, cot, codes, scales, out, act_v, cot_v, codes_v, scales_v, sems):
    rows = codes.shape[0]
    chunk = act.shape[1] // SIDE
    part = lambda k: pl.ds(k * chunk, chunk)
    copies = [
        pltpu.make_async_copy(cot, cot_v, sems.at[0]),
        pltpu.make_async_copy(codes, codes_v, sems.at[1]),
        pltpu.make_async_copy(scales, scales_v, sems.at[2]),
    ] + [
        pltpu.make_async_copy(act.at[:, part(k)], act_v.at[k], sems.at[3 + k]) for k in range(SIDE)
    ]
    for copy in copies:
        copy.start()
    x_first = lax.axis_index("rep") == 0
    copies[1].wait()
    copies[2].wait()
    weight = (codes_v[...].astype(jnp.float32) * scales_v[...]).astype(jnp.bfloat16)
    for peer in range(SIDE):
        out[peer, SIDE] = weight
    copies[0].wait()
    cot_t = cot_v[...].T
    for k in range(SIDE):
        copies[3 + k].wait()
        share = jnp.dot(cot_t, act_v[k], preferred_element_type=jnp.float32).astype(jnp.bfloat16)
        for j in range(SIDE):
            out[spot(x_first, k, j)] = share[:, j * rows : (j + 1) * rows]


def middle_kernel(blocks, out):
    for peer in range(SIDE):
        total = blocks[0, peer].astype(jnp.float32)
        for source in range(1, SIDE):
            total += blocks[source, peer].astype(jnp.float32)
        out[peer, SIDE] = total.astype(jnp.bfloat16)
        for source in range(SIDE):
            out[peer, source] = blocks[source, SIDE]


def keyvals_kernel(act, blocks, out, grad, weight):
    rows = blocks.shape[2]
    chunk = SIDE * rows
    z_last = lax.axis_index("rep") == 1
    total = None
    for k in range(SIDE):
        for j in range(SIDE):
            weight[pl.ds((k * SIDE + j) * rows, rows)] = blocks[spot(z_last, k, j)]
        part = pl.ds(k * chunk, chunk)
        product = jnp.dot(act[:, part], weight[part], preferred_element_type=jnp.float32)
        total = product if total is None else total + product
    out[...] = total.astype(jnp.bfloat16)
    share = blocks[0, SIDE].astype(jnp.float32)
    for peer in range(1, SIDE):
        share += blocks[peer, SIDE].astype(jnp.float32)
    grad[...] = share.T


def body(act, codes, scales, cotangent):
    tokens, width = act.shape
    rows, columns = codes.shape
    packed = (SIDE, SIDE + 1, columns, rows)
    vmem, hbm = pl.BlockSpec(memory_space=pltpu.VMEM), pl.BlockSpec(memory_space=pltpu.HBM)
    flops = 2 * tokens * width * columns
    cost = pl.CostEstimate(flops=flops, bytes_accessed=2 * act.size, transcendentals=0)
    exchange = lambda blocks, groups: lax.all_to_all(blocks, AXES, 0, 0, axis_index_groups=groups)

    sent = pl.pallas_call(
        grad_kernel,
        out_shape=jax.ShapeDtypeStruct(packed, jnp.bfloat16),
        in_specs=[hbm] * 4,
        out_specs=vmem,
        scratch_shapes=[
            pltpu.VMEM((SIDE, tokens, width // SIDE), act.dtype),
            pltpu.VMEM(cotangent.shape, cotangent.dtype),
            pltpu.VMEM(codes.shape, codes.dtype),
            pltpu.VMEM(scales.shape, scales.dtype),
            pltpu.SemaphoreType.DMA((3 + SIDE,)),
        ],
        compiler_params=params(60),
        cost_estimate=cost,
    )(act, cotangent, codes, scales)
    arrived = exchange(sent, lines(0))
    sent = pl.pallas_call(
        middle_kernel,
        out_shape=jax.ShapeDtypeStruct(packed, jnp.bfloat16),
        in_specs=[vmem],
        out_specs=vmem,
        compiler_params=params(),
    )(arrived)
    arrived = exchange(sent, lines(1))
    return tuple(
        pl.pallas_call(
            keyvals_kernel,
            out_shape=(
                jax.ShapeDtypeStruct((tokens, columns), jnp.bfloat16),
                jax.ShapeDtypeStruct((rows, columns), jnp.float32),
            ),
            in_specs=[vmem, vmem],
            out_specs=(vmem, vmem),
            scratch_shapes=[pltpu.VMEM((width, columns), jnp.bfloat16)],
            compiler_params=params(),
            cost_estimate=cost,
        )(act, arrived)
    )


def solution(mesh):
    split = Mesh(mesh.devices.reshape(SIDE, SIDE, 8, 2), ("z", "x", "local", "rep"))
    rows, columns = ("z", "x"), ("local", "rep")
    in_specs = (P(rows, None), P(rows, columns), P(rows, columns), P(rows, columns))
    out_specs = (P(rows, columns), P(rows, columns))
    return jax.shard_map(body, mesh=split, in_specs=in_specs, out_specs=out_specs, check_vma=False)
```

time: 168 us -> 99.1 us (0.59)
  the two profiles are of different devices: /device:TPU:4 before, /device:TPU:80 now
where the time goes in v3:
time: 99.1 us; the launch traced here: 98.9 us
  blocking collectives  89.4 us (90%)
  Pallas kernels  8.84 us (9%)
    all_to_all x2, blocking collectives, body(): lax.all_to_all(blocks, AXES, 0, 0, axis_index_groups=groups)  89.4 us
    pallas_call x1, Pallas kernels, body(): pl.pallas_call(grad_kernel, out_shape=jax.ShapeDtypeStruct(packed, jnp.bf...  5.37 us
    pallas_call x1, Pallas kernels, body(): pl.pallas_call(keyvals_kernel, out_shape=(jax.ShapeDtypeStruct((tokens, c...  3.19 us

profile of v3, /device:TPU:80, one launch (start us, length us, event | category | flops | bytes accessed | tf_op | source)
XLA Modules:
  0.0 98.9 jit_solution(13892793057872498818)
XLA Ops:
  0.6 5.4 %shard_map.59 = bf16[8,9,128,128]{3,2,1,0:T(8,128)(2,1)} custom-call(bf16[512,8192]{1,0:T(8,128)(2,1)} %act.3, bf16[512,128]{1,0:T(8,128)(2,1)} %cot.1, bf16[128,128]{1,0:T(8,128)(2,1)} %codes.1, f32[1,128]{1,0:T(1,128)} %scales.1), custom_call_target="tpu_custom_call" | custom-call | flops 1073741824 | bytes 8388608 | tf_op jit(solution)/shard_map/pallas_call | solution.py:94
  6.0 39.7 %all_to_all.10.blocks = bf16[8,9,128,128]{3,2,1,0:T(8,128)(2,1)S(1)} all-to-all(bf16[8,9,128,128]{3,2,1,0:T(8,128)(2,1)} %shard_map.59), channel_id=1, replica_groups={{0,16,32,48,64,80,96,112},{128,144,160,176,192,208,224,240},{256,272,28..., dimensions={0} | all-to-all | bytes 4718592 | tf_op jit(solution)/shard_map/all_to_all | solution.py:92
  45.7 0.0 copy-start
  45.7 0.3 shard_map.60
  46.0 49.7 %all_to_all.11.blocks = bf16[8,9,128,128]{3,2,1,0:T(8,128)(2,1)S(1)} all-to-all(bf16[8,9,128,128]{3,2,1,0:T(8,128)(2,1)S(1)} %shard_map.60), channel_id=1, replica_groups={{1,17,33,49,65,81,97,113},{129,145,161,177,193,209,225,241},{257,273,28..., dimensions={0} | all-to-all | bytes 4718592 | tf_op jit(solution)/shard_map/all_to_all | solution.py:92
  95.7 0.0 copy-done
  95.7 3.2 %shard_map.61 = (bf16[512,128]{1,0:T(8,128)(2,1)}, f32[128,128]{1,0:T(8,128)}) custom-call(bf16[512,8192]{1,0:T(8,128)(2,1)S(1)} %copy-done, bf16[8,9,128,128]{3,2,1,0:T(8,128)(2,1)S(1)} %all_to_all.11.blocks), custom_call_target="tpu_custom_call" | custom-call | flops 1073741824 | bytes 8388608 | tf_op jit(solution)/shard_map/pallas_call | solution.py:119
Async XLA Ops:
  45.7 50.0 %copy-start = (bf16[512,8192]{1,0:T(8,128)(2,1)S(1)}, bf16[512,8192]{1,0:T(8,128)(2,1)}, u32[]{:S(2)}) copy-start(bf16[512,8192]{1,0:T(8,128)(2,1)} %act.3) | copy-start | bytes 25165828

commit v4 on v0

v4 whole, which is shorter than its diff:
```python
import functools

import jax
import jax.numpy as jnp
from jax import lax
from jax.experimental import pallas as pl
from jax.experimental.pallas import tpu as pltpu
from jax.sharding import Mesh, PartitionSpec as P

SIDE = 8
TIED = 6
AXES = ("z", "x", "rep")


def lines(first):
    at = lambda z, x, r: (z * SIDE + x) * 2 + r
    along_x = [[at(z, x, first) for x in range(SIDE)] for z in range(SIDE)]
    along_z = [[at(z, x, 1 - first) for z in range(SIDE)] for x in range(SIDE)]
    return along_x + along_z


def steps(first, away):
    return [(line[i], line[(i + away) % SIDE]) for line in lines(first) for i in range(SIDE)]


def params(mib=32):
    return pltpu.CompilerParams(vmem_limit_bytes=mib * 1024 * 1024)


def spot(first, outer, inner):
    return jnp.where(first, inner, outer), jnp.where(first, outer, inner)


def weight_kernel(codes, scales, out):
    weight = (codes[...].astype(jnp.float32) * scales[...]).astype(jnp.bfloat16)
    for peer in range(SIDE):
        out[peer] = weight


def grad_kernel(act, cot, out, act_v, cot_v, sems):
    rows = out.shape[3]
    chunk = SIDE * rows
    copies = [pltpu.make_async_copy(cot, cot_v, sems.at[SIDE])] + [
        pltpu.make_async_copy(act.at[:, pl.ds(k * chunk, chunk)], act_v.at[k], sems.at[k])
        for k in range(SIDE)
    ]
    for copy in copies:
        copy.start()
    x_first = lax.axis_index("rep") == 0
    copies[0].wait()
    cot_t = cot_v[...].T
    for k in range(SIDE):
        copies[1 + k].wait()
        share = jnp.dot(cot_t, act_v[k], preferred_element_type=jnp.float32).astype(jnp.bfloat16)
        for j in range(SIDE):
            out[spot(x_first, k, j)] = share[:, j * rows : (j + 1) * rows]


def sum_of(blocks, *rest):
    total = blocks[(0, *rest)].astype(jnp.float32)
    for source in range(1, SIDE):
        total += blocks[(source, *rest)].astype(jnp.float32)
    return total


def middle_kernel(blocks, out):
    for peer in range(SIDE):
        out[peer] = sum_of(blocks, peer).astype(jnp.bfloat16)


def last_kernel(blocks, out):
    out[...] = sum_of(blocks).T


def keyvals_kernel(act, *refs):
    lines_of, (out, act_v, weight, sems) = refs[:SIDE], refs[SIDE:]
    rows = lines_of[0].shape[1]
    chunk = SIDE * rows
    copies = [
        pltpu.make_async_copy(act.at[:, pl.ds(k * chunk, chunk)], act_v.at[k], sems.at[k])
        for k in range(SIDE)
    ]
    for copy in copies:
        copy.start()
    z_last = lax.axis_index("rep") == 0
    me = jnp.where(z_last, lax.axis_index("z"), lax.axis_index("x"))
    for away, line in enumerate(lines_of):
        origin = lax.rem(me + (SIDE - away), SIDE)
        for j in range(SIDE):
            row = jnp.where(z_last, origin * SIDE + j, j * SIDE + origin) * rows
            weight[pl.ds(pl.multiple_of(row, rows), rows)] = line[j]
    total = None
    for k in range(SIDE):
        copies[k].wait()
        product = jnp.dot(
            act_v[k], weight[pl.ds(k * chunk, chunk)], preferred_element_type=jnp.float32
        )
        total = product if total is None else total + product
    out[...] = total.astype(jnp.bfloat16)


def local(kernel, out, args, mib=32, hbm=0, scratch=(), flops=0):
    vmem, far = pl.BlockSpec(memory_space=pltpu.VMEM), pl.BlockSpec(memory_space=pltpu.HBM)
    moved = sum(x.size * x.dtype.itemsize for x in (*args, out))
    return pl.pallas_call(
        kernel,
        out_shape=out,
        in_specs=[far] * hbm + [vmem] * (len(args) - hbm),
        out_specs=vmem,
        scratch_shapes=list(scratch),
        compiler_params=params(mib),
        cost_estimate=pl.CostEstimate(flops=flops, bytes_accessed=moved, transcendentals=0),
    )(*args)


def body(act, codes, scales, cotangent):
    tokens, width = act.shape
    rows, columns = codes.shape
    flops = 2 * tokens * width * columns
    bf16 = lambda *shape: jax.ShapeDtypeStruct(shape, jnp.bfloat16)
    one, all_of = bf16(SIDE, rows, columns), bf16(SIDE, SIDE, columns, rows)
    exchange = lambda blocks, groups: lax.all_to_all(blocks, AXES, 0, 0, axis_index_groups=groups)

    line = exchange(local(weight_kernel, one, (codes, scales)), lines(0))
    shares = local(
        grad_kernel,
        all_of,
        (act, cotangent),
        mib=60,
        hbm=2,
        scratch=(
            pltpu.VMEM((SIDE, tokens, width // SIDE), act.dtype),
            pltpu.VMEM(cotangent.shape, cotangent.dtype),
            pltpu.SemaphoreType.DMA((1 + SIDE,)),
        ),
        flops=flops,
    )
    shares = exchange(shares, lines(0))
    weights = [line] + [lax.ppermute(line, AXES, steps(1, away)) for away in range(1, SIDE)]
    shares, *weights[1:TIED] = lax.optimization_barrier((shares, *weights[1:TIED]))
    shares = exchange(local(middle_kernel, one, (shares,)), lines(1))
    keyvals = local(
        keyvals_kernel,
        bf16(tokens, columns),
        (act, *weights),
        mib=51,
        hbm=1,
        scratch=(
            pltpu.VMEM((SIDE, tokens, width // SIDE), act.dtype),
            pltpu.VMEM((width, columns), jnp.bfloat16),
            pltpu.SemaphoreType.DMA((SIDE,)),
        ),
        flops=flops,
    )
    grad = local(last_kernel, jax.ShapeDtypeStruct((rows, columns), jnp.float32), (shares,))
    return keyvals, grad


def solution(mesh):
    split = Mesh(mesh.devices.reshape(SIDE, SIDE, 8, 2), ("z", "x", "local", "rep"))
    rows, columns = ("z", "x"), ("local", "rep")
    in_specs = (P(rows, None), P(rows, columns), P(rows, columns), P(rows, columns))
    out_specs = (P(rows, columns), P(rows, columns))
    return jax.shard_map(body, mesh=split, in_specs=in_specs, out_specs=out_specs, check_vma=False)
```

time: 379 us -> 115 us (0.30)
  the two profiles are of different devices: /device:TPU:4 before, /device:TPU:36 now
where the time goes in v4:
time: 115 us; the launch traced here: 114 us
  starting transfers between devices  61.3 us (53%)
  waiting for transfers between devices  34.3 us (30%)
  Pallas kernels  14.9 us (13%)
  local copies, waits for them, and re-layouts  3.07 us (3%)
    ppermute x7, starting transfers between devices, body(): lax.ppermute(line, AXES, steps(1, away))  43.2 us
    ppermute x7, waiting for transfers between devices, body(): lax.ppermute(line, AXES, steps(1, away))  31.8 us
    all_to_all x3, starting transfers between devices, body(): lax.all_to_all(blocks, AXES, 0, 0, axis_index_groups=groups)  18.1 us
    pallas_call x5, Pallas kernels, local(): pl.pallas_call(kernel, out_shape=out, in_specs=[far] * hbm + [vmem] * (le...  14.9 us
    unnamed x8, local copies, waits for them, and re-layouts  3.07 us
    all_to_all x3, waiting for transfers between devices, body(): lax.all_to_all(blocks, AXES, 0, 0, axis_index_groups=groups)  2.49 us
  transfers between devices with their start and end apart: 10, of which 6 were waited for; matrix products, arithmetic and copies ran while one was open for 0% of the time, Pallas kernels for 11%

profile of v4, /device:TPU:36, one launch (start us, length us, event | category | flops | bytes accessed | tf_op | source)
XLA Modules:
  0.0 114.4 jit_solution(2674183259914113459)
XLA Ops:
  0.6 0.0 copy-start.2
  0.6 0.7 copy-done.2
  1.4 0.0 copy-start.3
  1.4 0.7 copy-done.3
  2.0 0.7 shard_map.59
  2.8 7.3 %all-to-all-start = ((bf16[8,128,128]{2,1,0:T(8,128)(2,1)}), bf16[8,128,128]{2,1,0:T(8,128)(2,1)S(1)}, u32[]{:S(2)}, u32[]{:S(2)}) async-start(bf16[8,128,128]{2,1,0:T(8,128)(2,1)} %shard_map.59), calls=%async_computation | async-start | bytes 524288 | tf_op jit(solution)/shard_map/all_to_all | solution.py:122
  10.0 5.2 %shard_map.60 = bf16[8,8,128,128]{3,2,1,0:T(8,128)(2,1)} custom-call(bf16[512,8192]{1,0:T(8,128)(2,1)} %act.3, bf16[512,128]{1,0:T(8,128)(2,1)} %cot.1), custom_call_target="tpu_custom_call" | custom-call | flops 1073741824 | bytes 10616832 | tf_op jit(solution)/shard_map/pallas_call | solution.py:105
  15.3 2.5 %all-to-all-done.refs_0_ = bf16[8,128,128]{2,1,0:T(8,128)(2,1)S(1)} async-done(((bf16[8,128,128]{2,1,0:T(8,128)(2,1)}), bf16[8,128,128]{2,1,0:T(8,128)(2,1)S(1)}, u32[]{:S(2)}, u32[]{:S(2)}) %all-to-all-start) | async-done | bytes 262176 | tf_op jit(solution)/shard_map/all_to_all | solution.py:122
  17.8 6.3 %all-to-all-start.1 = ((bf16[8,8,128,128]{3,2,1,0:T(8,128)(2,1)}), bf16[8,8,128,128]{3,2,1,0:T(8,128)(2,1)S(1)}, u32[]{:S(2)}, u32[]{:S(2)}) async-start(bf16[8,8,128,128]{3,2,1,0:T(8,128)(2,1)} %shard_map.60), calls=%async_computation.1 | async-start | bytes 4194304 | tf_op jit(solution)/shard_map/all_to_all | solution.py:122
  24.0 5.2 %collective-permute-start = (bf16[8,128,128]{2,1,0:T(8,128)(2,1)S(1)}, bf16[8,128,128]{2,1,0:T(8,128)(2,1)S(1)}, u32[]{:S(2)}, u32[]{:S(2)}) collective-permute-start(bf16[8,128,128]{2,1,0:T(8,128)(2,1)S(1)} %all-to-all-done.refs_0_), channel_id=1, source_target_pairs={{1,17},{17,33},{33,49},{49,65},{65,81},{81,97},{97,113},{113,1},{1... | collective-permute-start | bytes 786440 | tf_op jit(solution)/shard_map/ppermute | solution.py:139
  29.2 7.9 %collective-permute-start.1 = (bf16[8,128,128]{2,1,0:T(8,128)(2,1)S(1)}, bf16[8,128,128]{2,1,0:T(8,128)(2,1)S(1)}, u32[]{:S(2)}, u32[]{:S(2)}) collective-permute-start(bf16[8,128,128]{2,1,0:T(8,128)(2,1)S(1)} %all-to-all-done.refs_0_), channel_id=1, source_target_pairs={{1,33},{17,49},{33,65},{49,81},{65,97},{81,113},{97,1},{113,17},{1... | collective-permute-start | bytes 786440 | tf_op jit(solution)/shard_map/ppermute | solution.py:139
  37.1 10.0 %collective-permute-start.2 = (bf16[8,128,128]{2,1,0:T(8,128)(2,1)S(1)}, bf16[8,128,128]{2,1,0:T(8,128)(2,1)S(1)}, u32[]{:S(2)}, u32[]{:S(2)}) collective-permute-start(bf16[8,128,128]{2,1,0:T(8,128)(2,1)S(1)} %all-to-all-done.refs_0_), channel_id=1, source_target_pairs={{1,49},{17,65},{33,81},{49,97},{65,113},{81,1},{97,17},{113,33},{1... | collective-permute-start | bytes 786440 | tf_op jit(solution)/shard_map/ppermute | solution.py:139
  47.2 3.7 %collective-permute-start.3 = (bf16[8,128,128]{2,1,0:T(8,128)(2,1)S(1)}, bf16[8,128,128]{2,1,0:T(8,128)(2,1)S(1)}, u32[]{:S(2)}, u32[]{:S(2)}) collective-permute-start(bf16[8,128,128]{2,1,0:T(8,128)(2,1)S(1)} %all-to-all-done.refs_0_), channel_id=1, source_target_pairs={{1,65},{17,81},{33,97},{49,113},{65,1},{81,17},{97,33},{113,49},{1... | collective-permute-start | bytes 786440 | tf_op jit(solution)/shard_map/ppermute | solution.py:139
  50.9 6.9 %collective-permute-start.4 = (bf16[8,128,128]{2,1,0:T(8,128)(2,1)S(1)}, bf16[8,128,128]{2,1,0:T(8,128)(2,1)S(1)}, u32[]{:S(2)}, u32[]{:S(2)}) collective-permute-start(bf16[8,128,128]{2,1,0:T(8,128)(2,1)S(1)} %all-to-all-done.refs_0_), channel_id=1, source_target_pairs={{1,81},{17,97},{33,113},{49,1},{65,17},{81,33},{97,49},{113,65},{1... | collective-permute-start | bytes 786440 | tf_op jit(solution)/shard_map/ppermute | solution.py:139
  57.9 0.0 collective-permute-done.refs_1_
  57.9 7.8 %collective-permute-done.1.refs_2_ = bf16[8,128,128]{2,1,0:T(8,128)(2,1)S(1)} collective-permute-done((bf16[8,128,128]{2,1,0:T(8,128)(2,1)S(1)}, bf16[8,128,128]{2,1,0:T(8,128)(2,1)S(1)}, u32[]{:S(2)}, u32[]{:S(2)}) %collective-permute-start.1) | collective-permute-done | bytes 262176 | tf_op jit(solution)/shard_map/ppermute | solution.py:139
  65.7 6.3 %collective-permute-done.2.refs_3_ = bf16[8,128,128]{2,1,0:T(8,128)(2,1)S(1)} collective-permute-done((bf16[8,128,128]{2,1,0:T(8,128)(2,1)S(1)}, bf16[8,128,128]{2,1,0:T(8,128)(2,1)S(1)}, u32[]{:S(2)}, u32[]{:S(2)}) %collective-permute-start.2) | collective-permute-done | bytes 262176 | tf_op jit(solution)/shard_map/ppermute | solution.py:139
  72.0 11.6 %collective-permute-done.3.refs_4_ = bf16[8,128,128]{2,1,0:T(8,128)(2,1)S(1)} collective-permute-done((bf16[8,128,128]{2,1,0:T(8,128)(2,1)S(1)}, bf16[8,128,128]{2,1,0:T(8,128)(2,1)S(1)}, u32[]{:S(2)}, u32[]{:S(2)}) %collective-permute-start.3) | collective-permute-done | bytes 262176 | tf_op jit(solution)/shard_map/ppermute | solution.py:139
  83.5 0.0 collective-permute-done.4.refs_5_
  83.5 0.0 copy-start
  83.5 0.7 copy-done
  84.2 0.0 all-to-all-done.1.blocks
  84.2 1.0 shard_map.62
  85.2 4.6 %all-to-all-start.2 = ((bf16[8,128,128]{2,1,0:T(8,128)(2,1)}), bf16[8,128,128]{2,1,0:T(8,128)(2,1)S(1)}, u32[]{:S(2)}, u32[]{:S(2)}) async-start(bf16[8,128,128]{2,1,0:T(8,128)(2,1)} %shard_map.62), calls=%async_computation.2 | async-start | bytes 524288 | tf_op jit(solution)/shard_map/all_to_all | solution.py:122
  89.8 6.0 %collective-permute-start.5 = (bf16[8,128,128]{2,1,0:T(8,128)(2,1)S(1)}, bf16[8,128,128]{2,1,0:T(8,128)(2,1)S(1)}, u32[]{:S(2)}, u32[]{:S(2)}) collective-permute-start(bf16[8,128,128]{2,1,0:T(8,128)(2,1)S(1)} %all-to-all-done.refs_0_), channel_id=1, source_target_pairs={{1,97},{17,113},{33,1},{49,17},{65,33},{81,49},{97,65},{113,81},{1... | collective-permute-start | bytes 786440 | tf_op jit(solution)/shard_map/ppermute | solution.py:139
  95.9 3.4 %collective-permute-start.6 = (bf16[8,128,128]{2,1,0:T(8,128)(2,1)S(1)}, bf16[8,128,128]{2,1,0:T(8,128)(2,1)S(1)}, u32[]{:S(2)}, u32[]{:S(2)}) collective-permute-start(bf16[8,128,128]{2,1,0:T(8,128)(2,1)S(1)} %all-to-all-done.refs_0_), channel_id=1, source_target_pairs={{1,113},{17,1},{33,17},{49,33},{65,49},{81,65},{97,81},{113,97},{1... | collective-permute-start | bytes 786440 | tf_op jit(solution)/shard_map/ppermute | solution.py:139
  99.2 4.0 %collective-permute-done.5.refs_6_ = bf16[8,128,128]{2,1,0:T(8,128)(2,1)S(1)} collective-permute-done((bf16[8,128,128]{2,1,0:T(8,128)(2,1)S(1)}, bf16[8,128,128]{2,1,0:T(8,128)(2,1)S(1)}, u32[]{:S(2)}, u32[]{:S(2)}) %collective-permute-start.5) | collective-permute-done | bytes 262176 | tf_op jit(solution)/shard_map/ppermute | solution.py:139
  103.2 2.2 %collective-permute-done.6.refs_7_ = bf16[8,128,128]{2,1,0:T(8,128)(2,1)S(1)} collective-permute-done((bf16[8,128,128]{2,1,0:T(8,128)(2,1)S(1)}, bf16[8,128,128]{2,1,0:T(8,128)(2,1)S(1)}, u32[]{:S(2)}, u32[]{:S(2)}) %collective-permute-start.6) | collective-permute-done | bytes 262176 | tf_op jit(solution)/shard_map/ppermute | solution.py:139
  105.4 0.0 copy-start.1
  105.4 0.9 copy-done.1
  106.4 7.2 %shard_map.61 = bf16[512,128]{1,0:T(8,128)(2,1)} custom-call(bf16[512,8192]{1,0:T(8,128)(2,1)} %act.3, bf16[8,128,128]{2,1,0:T(8,128)(2,1)S(1)} %all-to-all-done.refs_0_, bf16[8,128,128]{2,1,0:T(8,128)(2,1)S(1)} %collective-permute-done.refs_1_, bf16[8,128,128]{2,1,0:T(8,128)(2,1)S(1)} %collective-permute-done.1.refs_2_, ...), custom_call_target="tpu_custom_call" | custom-call | flops 1073741824 | bytes 10616832 | tf_op jit(solution)/shard_map/pallas_call | solution.py:105
  113.6 0.0 all-to-all-done.2.blocks
  113.6 0.7 shard_map.63
Async XLA Ops:
  0.6 0.8 copy-start.2
  1.4 0.7 copy-start.3
  2.8 15.0 %all-to-all-start = ((bf16[8,128,128]{2,1,0:T(8,128)(2,1)}), bf16[8,128,128]{2,1,0:T(8,128)(2,1)S(1)}, u32[]{:S(2)}, u32[]{:S(2)}) async-start(bf16[8,128,128]{2,1,0:T(8,128)(2,1)} %shard_map.59), calls=%async_computation | async-start | bytes 524288 | tf_op jit(solution)/shard_map/all_to_all | solution.py:122
  17.8 66.5 %all-to-all-start.1 = ((bf16[8,8,128,128]{3,2,1,0:T(8,128)(2,1)}), bf16[8,8,128,128]{3,2,1,0:T(8,128)(2,1)S(1)}, u32[]{:S(2)}, u32[]{:S(2)}) async-start(bf16[8,8,128,128]{3,2,1,0:T(8,128)(2,1)} %shard_map.60), calls=%async_computation.1 | async-start | bytes 4194304 | tf_op jit(solution)/shard_map/all_to_all | solution.py:122
  24.0 33.8 %collective-permute-start = (bf16[8,128,128]{2,1,0:T(8,128)(2,1)S(1)}, bf16[8,128,128]{2,1,0:T(8,128)(2,1)S(1)}, u32[]{:S(2)}, u32[]{:S(2)}) collective-permute-start(bf16[8,128,128]{2,1,0:T(8,128)(2,1)S(1)} %all-to-all-done.refs_0_), channel_id=1, source_target_pairs={{1,17},{17,33},{33,49},{49,65},{65,81},{81,97},{97,113},{113,1},{1... | collective-permute-start | bytes 786440 | tf_op jit(solution)/shard_map/ppermute | solution.py:139
  29.2 36.5 %collective-permute-start.1 = (bf16[8,128,128]{2,1,0:T(8,128)(2,1)S(1)}, bf16[8,128,128]{2,1,0:T(8,128)(2,1)S(1)}, u32[]{:S(2)}, u32[]{:S(2)}) collective-permute-start(bf16[8,128,128]{2,1,0:T(8,128)(2,1)S(1)} %all-to-all-done.refs_0_), channel_id=1, source_target_pairs={{1,33},{17,49},{33,65},{49,81},{65,97},{81,113},{97,1},{113,17},{1... | collective-permute-start | bytes 786440 | tf_op jit(solution)/shard_map/ppermute | solution.py:139
  37.1 34.8 %collective-permute-start.2 = (bf16[8,128,128]{2,1,0:T(8,128)(2,1)S(1)}, bf16[8,128,128]{2,1,0:T(8,128)(2,1)S(1)}, u32[]{:S(2)}, u32[]{:S(2)}) collective-permute-start(bf16[8,128,128]{2,1,0:T(8,128)(2,1)S(1)} %all-to-all-done.refs_0_), channel_id=1, source_target_pairs={{1,49},{17,65},{33,81},{49,97},{65,113},{81,1},{97,17},{113,33},{1... | collective-permute-start | bytes 786440 | tf_op jit(solution)/shard_map/ppermute | solution.py:139
  47.2 36.3 %collective-permute-start.3 = (bf16[8,128,128]{2,1,0:T(8,128)(2,1)S(1)}, bf16[8,128,128]{2,1,0:T(8,128)(2,1)S(1)}, u32[]{:S(2)}, u32[]{:S(2)}) collective-permute-start(bf16[8,128,128]{2,1,0:T(8,128)(2,1)S(1)} %all-to-all-done.refs_0_), channel_id=1, source_target_pairs={{1,65},{17,81},{33,97},{49,113},{65,1},{81,17},{97,33},{113,49},{1... | collective-permute-start | bytes 786440 | tf_op jit(solution)/shard_map/ppermute | solution.py:139
  50.9 32.6 %collective-permute-start.4 = (bf16[8,128,128]{2,1,0:T(8,128)(2,1)S(1)}, bf16[8,128,128]{2,1,0:T(8,128)(2,1)S(1)}, u32[]{:S(2)}, u32[]{:S(2)}) collective-permute-start(bf16[8,128,128]{2,1,0:T(8,128)(2,1)S(1)} %all-to-all-done.refs_0_), channel_id=1, source_target_pairs={{1,81},{17,97},{33,113},{49,1},{65,17},{81,33},{97,49},{113,65},{1... | collective-permute-start | bytes 786440 | tf_op jit(solution)/shard_map/ppermute | solution.py:139
  83.5 0.7 copy-start
  85.2 28.4 %all-to-all-start.2 = ((bf16[8,128,128]{2,1,0:T(8,128)(2,1)}), bf16[8,128,128]{2,1,0:T(8,128)(2,1)S(1)}, u32[]{:S(2)}, u32[]{:S(2)}) async-start(bf16[8,128,128]{2,1,0:T(8,128)(2,1)} %shard_map.62), calls=%async_computation.2 | async-start | bytes 524288 | tf_op jit(solution)/shard_map/all_to_all | solution.py:122
  89.8 13.4 %collective-permute-start.5 = (bf16[8,128,128]{2,1,0:T(8,128)(2,1)S(1)}, bf16[8,128,128]{2,1,0:T(8,128)(2,1)S(1)}, u32[]{:S(2)}, u32[]{:S(2)}) collective-permute-start(bf16[8,128,128]{2,1,0:T(8,128)(2,1)S(1)} %all-to-all-done.refs_0_), channel_id=1, source_target_pairs={{1,97},{17,113},{33,1},{49,17},{65,33},{81,49},{97,65},{113,81},{1... | collective-permute-start | bytes 786440 | tf_op jit(solution)/shard_map/ppermute | solution.py:139
  95.9 9.6 %collective-permute-start.6 = (bf16[8,128,128]{2,1,0:T(8,128)(2,1)S(1)}, bf16[8,128,128]{2,1,0:T(8,128)(2,1)S(1)}, u32[]{:S(2)}, u32[]{:S(2)}) collective-permute-start(bf16[8,128,128]{2,1,0:T(8,128)(2,1)S(1)} %all-to-all-done.refs_0_), channel_id=1, source_target_pairs={{1,113},{17,1},{33,17},{49,33},{65,49},{81,65},{97,81},{113,97},{1... | collective-permute-start | bytes 786440 | tf_op jit(solution)/shard_map/ppermute | solution.py:139
  105.4 1.0 copy-start.1

commit v5 on v4

v5 whole, which is shorter than its diff:
```python
import jax
import jax.numpy as jnp
from jax import lax
from jax.experimental import pallas as pl
from jax.experimental.pallas import tpu as pltpu
from jax.sharding import Mesh, PartitionSpec as P

SIDE = 8
HALF = SIDE // 2
AXES = ("z", "x", "rep")


def lines(first):
    at = lambda z, x, r: (z * SIDE + x) * 2 + r
    along_x = [[at(z, x, first) for x in range(SIDE)] for z in range(SIDE)]
    along_z = [[at(z, x, 1 - first) for z in range(SIDE)] for x in range(SIDE)]
    return along_x + along_z


def halves():
    return [line[parity::2] for line in lines(1) for parity in range(2)]


def shift(x, away):
    pairs = [(line[i], line[(i + away) % SIDE]) for line in lines(1) for i in range(SIDE)]
    return lax.ppermute(x, AXES, pairs)


def place():
    along_z = lax.axis_index("rep") == 0
    return along_z, jnp.where(along_z, lax.axis_index("z"), lax.axis_index("x"))


def weight_kernel(codes, scales, out):
    weight = (codes[...].astype(jnp.float32) * scales[...]).astype(jnp.bfloat16)
    for peer in range(SIDE):
        out[peer] = weight


def grad_kernel(act, cot, keep, up, down, act_v, cot_v, out_v, sems):
    rows = keep.shape[3]
    chunk = SIDE * rows
    copies = [pltpu.make_async_copy(cot, cot_v, sems.at[SIDE])] + [
        pltpu.make_async_copy(act.at[:, pl.ds(k * chunk, chunk)], act_v.at[k], sems.at[k])
        for k in range(SIDE)
    ]
    for copy in copies:
        copy.start()
    along_z, me = place()
    copies[0].wait()
    cot_t = cot_v[...].T
    for k in range(SIDE):
        copies[1 + k].wait()
        share = jnp.dot(cot_t, act_v[k], preferred_element_type=jnp.float32).astype(jnp.bfloat16)
        for j in range(SIDE):
            away = lax.rem(jnp.where(along_z, k, j) - me + SIDE, SIDE)
            odd = jnp.where(away < HALF, HALF + away // 2, SIDE + 1 - away // 2)
            slot = jnp.where(lax.rem(away, 2) == 0, away // 2, odd)
            out_v[slot, jnp.where(along_z, j, k)] = share[:, j * rows : (j + 1) * rows]
    back = [
        pltpu.make_async_copy(out_v.at[pl.ds(0, HALF)], keep, sems.at[0]),
        pltpu.make_async_copy(out_v.at[pl.ds(HALF, 2)], up, sems.at[1]),
        pltpu.make_async_copy(out_v.at[pl.ds(HALF + 2, 2)], down, sems.at[2]),
    ]
    for copy in back:
        copy.start()
    for copy in back:
        copy.wait()


def combine_kernel(keep, below, above, line, out):
    me = place()[1] // 2
    wide = lambda block: block.astype(jnp.float32)
    for even in range(HALF):
        peer = lax.rem(me + even, HALF)
        for j in range(SIDE):
            total = wide(keep[even, j])
            if even < 2:
                total += wide(below[even, j])
            if even in (0, HALF - 1):
                total += wide(above[min(even, 1), j])
            out[peer, j] = total.astype(jnp.bfloat16)
        out[even, pl.ds(SIDE, SIDE)] = line[...]


def middle_kernel(blocks, out, up, down):
    me = place()[1] // 2
    for j in range(SIDE):
        total = blocks[0, j].astype(jnp.float32)
        for source in range(1, HALF):
            total += blocks[source, j].astype(jnp.float32)
        out[j] = total.astype(jnp.bfloat16)
    mine = lambda step: blocks[lax.rem(me + step, HALF), pl.ds(SIDE, SIDE)]
    up[0] = down[0] = mine(0)
    up[1] = mine(HALF - 1)
    down[1] = mine(1)


def keyvals_kernel(act, blocks, below, above, out, weight):
    rows = blocks.shape[2]
    chunk = SIDE * rows
    along_z, me = place()

    def put(origin, read):
        for j in range(SIDE):
            row = jnp.where(along_z, origin * SIDE + j, j * SIDE + origin) * rows
            weight[pl.ds(pl.multiple_of(row, rows), rows)] = read(j)

    for half in range(HALF):
        put(lax.rem(me, 2) + 2 * half, lambda j: blocks[half, SIDE + j])
    for k in range(2):
        put(lax.rem(me + 1 + 2 * k, SIDE), lambda j: above[k, j])
        put(lax.rem(me + SIDE - 1 - 2 * k, SIDE), lambda j: below[k, j])
    total = None
    for k in range(SIDE):
        part = pl.ds(k * chunk, chunk)
        product = jnp.dot(act[:, part], weight[part], preferred_element_type=jnp.float32)
        total = product if total is None else total + product
    out[...] = total.astype(jnp.bfloat16)


def last_kernel(blocks, out):
    total = blocks[0].astype(jnp.float32)
    for source in range(1, SIDE):
        total += blocks[source].astype(jnp.float32)
    out[...] = total.T


def local(kernel, out, args, mib=32, far=False, scratch=(), flops=0):
    spec = pl.BlockSpec(memory_space=pltpu.HBM if far else pltpu.VMEM)
    moved = sum(x.size * x.dtype.itemsize for x in (*args, *jax.tree.leaves(out)))
    return pl.pallas_call(
        kernel,
        out_shape=out,
        in_specs=[spec] * len(args),
        out_specs=jax.tree.map(lambda _: spec, out),
        scratch_shapes=list(scratch),
        compiler_params=pltpu.CompilerParams(vmem_limit_bytes=mib * 1024 * 1024),
        cost_estimate=pl.CostEstimate(flops=flops, bytes_accessed=moved, transcendentals=0),
    )(*args)


def body(act, codes, scales, cotangent):
    tokens, width = act.shape
    rows, columns = codes.shape
    flops = 2 * tokens * width * columns
    bf16 = lambda *shape: jax.ShapeDtypeStruct((*shape, columns, rows), jnp.bfloat16)
    one, two = bf16(SIDE), bf16(2, SIDE)
    exchange = lambda blocks, groups: lax.all_to_all(blocks, AXES, 0, 0, axis_index_groups=groups)

    line = exchange(local(weight_kernel, one, (codes, scales)), lines(0))
    keep, up, down = local(
        grad_kernel,
        (bf16(HALF, SIDE), two, two),
        (act, cotangent),
        mib=60,
        far=True,
        scratch=(
            pltpu.VMEM((SIDE, tokens, width // SIDE), act.dtype),
            pltpu.VMEM(cotangent.shape, cotangent.dtype),
            pltpu.VMEM((SIDE, SIDE, columns, rows), jnp.bfloat16),
            pltpu.SemaphoreType.DMA((1 + SIDE,)),
        ),
        flops=flops,
    )
    packed = local(
        combine_kernel, bf16(HALF, 2 * SIDE), (keep, shift(up, 1), shift(down, SIDE - 1), line)
    )
    blocks = exchange(packed, halves())
    shares, up, down = local(middle_kernel, (one, two, two), (blocks,))
    shares = exchange(shares, lines(0))
    keyvals = local(
        keyvals_kernel,
        jax.ShapeDtypeStruct((tokens, columns), jnp.bfloat16),
        (act, blocks, shift(up, 1), shift(down, SIDE - 1)),
        scratch=(pltpu.VMEM((width, columns), jnp.bfloat16),),
        flops=flops,
    )
    grad = local(last_kernel, jax.ShapeDtypeStruct((rows, columns), jnp.float32), (shares,))
    return keyvals, grad


def solution(mesh):
    split = Mesh(mesh.devices.reshape(SIDE, SIDE, 8, 2), ("z", "x", "local", "rep"))
    rows, columns = ("z", "x"), ("local", "rep")
    in_specs = (P(rows, None), P(rows, columns), P(rows, columns), P(rows, columns))
    out_specs = (P(rows, columns), P(rows, columns))
    return jax.shard_map(body, mesh=split, in_specs=in_specs, out_specs=out_specs, check_vma=False)
```

time: 115 us -> 101 us (0.88)
  the two profiles are of different devices: /device:TPU:36 before, /device:TPU:64 now
where the time goes in v5:
time: 101 us
  blocking collectives  63 us (62%)
  starting transfers between devices  26.3 us (26%)
  Pallas kernels  9.74 us (10%)
  local copies, waits for them, and re-layouts  1.24 us (1%)
    all_to_all x3, blocking collectives, body(): lax.all_to_all(blocks, AXES, 0, 0, axis_index_groups=groups)  63 us
    ppermute x4, starting transfers between devices, shift(): return lax.ppermute(x, AXES, pairs)  26.3 us
    pallas_call x6, Pallas kernels, local(): pl.pallas_call(kernel, out_shape=out, in_specs=[spec] * len(args), out_sp...  9.74 us
  transfers between devices with their start and end apart: 4, of which 0 were waited for; matrix products, arithmetic and copies ran while one was open for 0% of the time, Pallas kernels for 1%

profile of v5, /device:TPU:64, one launch (start us, length us, event | category | flops | bytes accessed | tf_op | source)
XLA Modules:
  0.0 101.0 jit_solution(4453158986262103675)
XLA Ops:
  0.6 0.0 copy-start.3
  0.6 0.0 copy-start.2
  0.7 5.3 %shard_map.59 = (bf16[4,8,128,128]{3,2,1,0:T(8,128)(2,1)}, bf16[2,8,128,128]{3,2,1,0:T(8,128)(2,1)}, bf16[2,8,128,128]{3,2,1,0:T(8,128)(2,1)}) custom-call(bf16[512,8192]{1,0:T(8,128)(2,1)} %act.3, bf16[512,128]{1,0:T(8,128)(2,1)} %cot.1), custom_call_target="tpu_custom_call" | custom-call | flops 1073741824 | bytes 10616832 | tf_op jit(solution)/shard_map/pallas_call | solution.py:132
  6.0 5.2 %collective-permute-start = (bf16[2,8,128,128]{3,2,1,0:T(8,128)(2,1)}, bf16[2,8,128,128]{3,2,1,0:T(8,128)(2,1)S(1)}, u32[]{:S(2)}, u32[]{:S(2)}) collective-permute-start(bf16[2,8,128,128]{3,2,1,0:T(8,128)(2,1)} %get-tuple-element.9), channel_id=1, source_target_pairs={{1,17},{17,33},{33,49},{49,65},{65,81},{81,97},{97,113},{113,1},{1... | collective-permute-start | bytes 1572872 | tf_op jit(solution)/shard_map/ppermute | solution.py:26
  11.2 14.0 %collective-permute-start.1 = (bf16[2,8,128,128]{3,2,1,0:T(8,128)(2,1)}, bf16[2,8,128,128]{3,2,1,0:T(8,128)(2,1)S(1)}, u32[]{:S(2)}, u32[]{:S(2)}) collective-permute-start(bf16[2,8,128,128]{3,2,1,0:T(8,128)(2,1)} %get-tuple-element.10), channel_id=1, source_target_pairs={{1,113},{17,1},{33,17},{49,33},{65,49},{81,65},{97,81},{113,97},{1... | collective-permute-start | bytes 1572872 | tf_op jit(solution)/shard_map/ppermute | solution.py:26
  25.2 0.0 copy-done.3
  25.2 0.0 copy-done.2
  25.3 17.1 %all_to_all.15.line = bf16[8,128,128]{2,1,0:T(8,128)(2,1)S(1)} all-to-all(bf16[8,128,128]{2,1,0:T(8,128)(2,1)S(1)} %shard_map.60), channel_id=1, replica_groups={{0,16,32,48,64,80,96,112},{128,144,160,176,192,208,224,240},{256,272,28..., dimensions={0} | all-to-all | bytes 524288 | tf_op jit(solution)/shard_map/all_to_all | solution.py:149
  42.4 0.0 collective-permute-done.below
  42.4 0.0 collective-permute-done.1.above
  42.4 0.0 copy-start.1
  42.4 1.2 %copy-done.1 = bf16[4,8,128,128]{3,2,1,0:T(8,128)(2,1)S(1)} copy-done((bf16[4,8,128,128]{3,2,1,0:T(8,128)(2,1)S(1)}, bf16[4,8,128,128]{3,2,1,0:T(8,128)(2,1)}, u32[]{:S(2)}) %copy-start.1) | copy-done | bytes 1048600
  43.6 0.0 copy-start
  43.6 0.3 shard_map.61
  43.9 33.0 %all_to_all.16.blocks = bf16[4,16,128,128]{3,2,1,0:T(8,128)(2,1)S(1)} all-to-all(bf16[4,16,128,128]{3,2,1,0:T(8,128)(2,1)S(1)} %shard_map.61), channel_id=1, replica_groups={{1,33,65,97},{17,49,81,113},{129,161,193,225},{145,177,209,241},{257,28..., dimensions={0} | all-to-all | bytes 4194304 | tf_op jit(solution)/shard_map/all_to_all | solution.py:149
  76.9 0.2 shard_map.62
  77.1 2.5 %collective-permute-start.2 = (bf16[2,8,128,128]{3,2,1,0:T(8,128)(2,1)S(1)}, bf16[2,8,128,128]{3,2,1,0:T(8,128)(2,1)S(1)}, u32[]{:S(2)}, u32[]{:S(2)}) collective-permute-start(bf16[2,8,128,128]{3,2,1,0:T(8,128)(2,1)S(1)} %get-tuple-element.11), channel_id=1, source_target_pairs={{1,17},{17,33},{33,49},{49,65},{65,81},{81,97},{97,113},{113,1},{1... | collective-permute-start | bytes 1572872 | tf_op jit(solution)/shard_map/ppermute | solution.py:26
  79.6 4.6 %collective-permute-start.3 = (bf16[2,8,128,128]{3,2,1,0:T(8,128)(2,1)S(1)}, bf16[2,8,128,128]{3,2,1,0:T(8,128)(2,1)S(1)}, u32[]{:S(2)}, u32[]{:S(2)}) collective-permute-start(bf16[2,8,128,128]{3,2,1,0:T(8,128)(2,1)S(1)} %get-tuple-element.12), channel_id=1, source_target_pairs={{1,113},{17,1},{33,17},{49,33},{65,49},{81,65},{97,81},{113,97},{1... | collective-permute-start | bytes 1572872 | tf_op jit(solution)/shard_map/ppermute | solution.py:26
  84.2 12.9 %all_to_all.17.blocks = bf16[8,128,128]{2,1,0:T(8,128)(2,1)S(1)} all-to-all(bf16[8,128,128]{2,1,0:T(8,128)(2,1)S(1)} %get-tuple-element.13), channel_id=1, replica_groups={{0,16,32,48,64,80,96,112},{128,144,160,176,192,208,224,240},{256,272,28..., dimensions={0} | all-to-all | bytes 524288 | tf_op jit(solution)/shard_map/all_to_all | solution.py:149
  97.1 0.7 shard_map.64
  97.8 0.0 collective-permute-done.2.below
  97.8 0.0 collective-permute-done.3.above
  97.8 0.0 copy-done
  97.8 3.1 %shard_map.63 = bf16[512,128]{1,0:T(8,128)(2,1)} custom-call(bf16[512,8192]{1,0:T(8,128)(2,1)S(1)} %copy-done, bf16[4,16,128,128]{3,2,1,0:T(8,128)(2,1)S(1)} %all_to_all.16.blocks, bf16[2,8,128,128]{3,2,1,0:T(8,128)(2,1)S(1)} %collective-permute-done.2.below, bf16[2,8,128,128]{3,2,1,0:T(8,128)(2,1)S(1)} %collective-permute-done.3.above), custom_call_target="tpu_custom_call" | custom-call | flops 1073741824 | bytes 11665408 | tf_op jit(solution)/shard_map/pallas_call | solution.py:132
  (1 shorter events, 0.0 us)
Async XLA Ops:
  0.6 24.6 %copy-start.3 = (f32[1,128]{1,0:T(1,128)S(1)}, f32[1,128]{1,0:T(1,128)}, u32[]{:S(2)}) copy-start(f32[1,128]{1,0:T(1,128)} %scales.1) | copy-start | bytes 1540
  0.6 24.6 %copy-start.2 = (bf16[128,128]{1,0:T(8,128)(2,1)S(1)}, bf16[128,128]{1,0:T(8,128)(2,1)}, u32[]{:S(2)}) copy-start(bf16[128,128]{1,0:T(8,128)(2,1)} %codes.1) | copy-start | bytes 98308
  6.0 36.4 %collective-permute-start = (bf16[2,8,128,128]{3,2,1,0:T(8,128)(2,1)}, bf16[2,8,128,128]{3,2,1,0:T(8,128)(2,1)S(1)}, u32[]{:S(2)}, u32[]{:S(2)}) collective-permute-start(bf16[2,8,128,128]{3,2,1,0:T(8,128)(2,1)} %get-tuple-element.9), channel_id=1, source_target_pairs={{1,17},{17,33},{33,49},{49,65},{65,81},{81,97},{97,113},{113,1},{1... | collective-permute-start | bytes 1572872 | tf_op jit(solution)/shard_map/ppermute | solution.py:26
  11.2 31.2 %collective-permute-start.1 = (bf16[2,8,128,128]{3,2,1,0:T(8,128)(2,1)}, bf16[2,8,128,128]{3,2,1,0:T(8,128)(2,1)S(1)}, u32[]{:S(2)}, u32[]{:S(2)}) collective-permute-start(bf16[2,8,128,128]{3,2,1,0:T(8,128)(2,1)} %get-tuple-element.10), channel_id=1, source_target_pairs={{1,113},{17,1},{33,17},{49,33},{65,49},{81,65},{97,81},{113,97},{1... | collective-permute-start | bytes 1572872 | tf_op jit(solution)/shard_map/ppermute | solution.py:26
  42.4 1.2 %copy-start.1 = (bf16[4,8,128,128]{3,2,1,0:T(8,128)(2,1)S(1)}, bf16[4,8,128,128]{3,2,1,0:T(8,128)(2,1)}, u32[]{:S(2)}) copy-start(bf16[4,8,128,128]{3,2,1,0:T(8,128)(2,1)} %get-tuple-element.8.keep) | copy-start | bytes 3145732
  43.6 54.2 %copy-start = (bf16[512,8192]{1,0:T(8,128)(2,1)S(1)}, bf16[512,8192]{1,0:T(8,128)(2,1)}, u32[]{:S(2)}) copy-start(bf16[512,8192]{1,0:T(8,128)(2,1)} %act.3) | copy-start | bytes 25165828
  77.1 20.7 %collective-permute-start.2 = (bf16[2,8,128,128]{3,2,1,0:T(8,128)(2,1)S(1)}, bf16[2,8,128,128]{3,2,1,0:T(8,128)(2,1)S(1)}, u32[]{:S(2)}, u32[]{:S(2)}) collective-permute-start(bf16[2,8,128,128]{3,2,1,0:T(8,128)(2,1)S(1)} %get-tuple-element.11), channel_id=1, source_target_pairs={{1,17},{17,33},{33,49},{49,65},{65,81},{81,97},{97,113},{113,1},{1... | collective-permute-start | bytes 1572872 | tf_op jit(solution)/shard_map/ppermute | solution.py:26
  79.6 18.2 %collective-permute-start.3 = (bf16[2,8,128,128]{3,2,1,0:T(8,128)(2,1)S(1)}, bf16[2,8,128,128]{3,2,1,0:T(8,128)(2,1)S(1)}, u32[]{:S(2)}, u32[]{:S(2)}) collective-permute-start(bf16[2,8,128,128]{3,2,1,0:T(8,128)(2,1)S(1)} %get-tuple-element.12), channel_id=1, source_target_pairs={{1,113},{17,1},{33,17},{49,33},{65,49},{81,65},{97,81},{113,97},{1... | collective-permute-start | bytes 1572872 | tf_op jit(solution)/shard_map/ppermute | solution.py:26

commit v6 on v5

--- a/solution.py
+++ b/solution.py
@@ -163,6 +163,7 @@
         ),
         flops=flops,
     )
+    line, down = lax.optimization_barrier((line, down))
     packed = local(
         combine_kernel, bf16(HALF, 2 * SIDE), (keep, shift(up, 1), shift(down, SIDE - 1), line)
     )
@@ -176,6 +177,7 @@
         scratch=(pltpu.VMEM((width, columns), jnp.bfloat16),),
         flops=flops,
     )
+    shares, keyvals = lax.optimization_barrier((shares, keyvals))
     grad = local(last_kernel, jax.ShapeDtypeStruct((rows, columns), jnp.float32), (shares,))
     return keyvals, grad
 

time: 101 us -> 105 us (1.040)
  the two profiles are of different devices: /device:TPU:64 before, /device:TPU:96 now
where the time goes in v6:
time: 105 us
  starting transfers between devices  42.1 us (40%)
  blocking collectives  33 us (31%)
  Pallas kernels  11.4 us (11%)
  waiting for transfers between devices  10.9 us (10%)
  local copies, waits for them, and re-layouts  6.73 us (6%)
    all_to_all x1, blocking collectives, body(): lax.all_to_all(blocks, AXES, 0, 0, axis_index_groups=groups)  33 us
    ppermute x4, starting transfers between devices, shift(): return lax.ppermute(x, AXES, pairs)  29.6 us
    all_to_all x2, starting transfers between devices, body(): lax.all_to_all(blocks, AXES, 0, 0, axis_index_groups=groups)  12.4 us
    pallas_call x6, Pallas kernels, local(): pl.pallas_call(kernel, out_shape=out, in_specs=[spec] * len(args), out_sp...  11.4 us
    ppermute x4, waiting for transfers between devices, shift(): return lax.ppermute(x, AXES, pairs)  10.8 us
    unnamed x10, local copies, waits for them, and re-layouts  6.73 us
  transfers between devices with their start and end apart: 6, of which 5 were waited for; matrix products, arithmetic and copies ran while one was open for 0% of the time, Pallas kernels for 8%

profile of v6, /device:TPU:96, one launch (start us, length us, event | category | flops | bytes accessed | tf_op | source)
XLA Modules:
  0.0 104.9 jit_solution(11922002728309017337)
XLA Ops:
  0.6 0.0 copy-start.3
  0.6 0.7 copy-done.3
  1.4 0.0 copy-start.4
  1.4 0.7 copy-done.4
  2.0 0.7 shard_map.60
  2.8 6.8 %all-to-all-start = ((bf16[8,128,128]{2,1,0:T(8,128)(2,1)}), bf16[8,128,128]{2,1,0:T(8,128)(2,1)S(1)}, u32[]{:S(2)}, u32[]{:S(2)}) async-start(bf16[8,128,128]{2,1,0:T(8,128)(2,1)} %shard_map.60), calls=%async_computation | async-start | bytes 524288 | tf_op jit(solution)/shard_map/all_to_all | solution.py:149
  9.5 5.3 %shard_map.59 = (bf16[4,8,128,128]{3,2,1,0:T(8,128)(2,1)}, bf16[2,8,128,128]{3,2,1,0:T(8,128)(2,1)}, bf16[2,8,128,128]{3,2,1,0:T(8,128)(2,1)}) custom-call(bf16[512,8192]{1,0:T(8,128)(2,1)} %act.3, bf16[512,128]{1,0:T(8,128)(2,1)} %cot.1), custom_call_target="tpu_custom_call" | custom-call | flops 1073741824 | bytes 10616832 | tf_op jit(solution)/shard_map/pallas_call | solution.py:132
  14.8 5.2 %collective-permute-start = (bf16[2,8,128,128]{3,2,1,0:T(8,128)(2,1)}, bf16[2,8,128,128]{3,2,1,0:T(8,128)(2,1)S(1)}, u32[]{:S(2)}, u32[]{:S(2)}) collective-permute-start(bf16[2,8,128,128]{3,2,1,0:T(8,128)(2,1)} %get-tuple-element.13), channel_id=1, source_target_pairs={{1,17},{17,33},{33,49},{49,65},{65,81},{81,97},{97,113},{113,1},{1... | collective-permute-start | bytes 1572872 | tf_op jit(solution)/shard_map/ppermute | solution.py:26
  20.0 0.0 all-to-all-done.line
  20.0 17.4 %collective-permute-start.1 = (bf16[2,8,128,128]{3,2,1,0:T(8,128)(2,1)}, bf16[2,8,128,128]{3,2,1,0:T(8,128)(2,1)S(1)}, u32[]{:S(2)}, u32[]{:S(2)}) collective-permute-start(bf16[2,8,128,128]{3,2,1,0:T(8,128)(2,1)} %get-tuple-element.15), channel_id=1, source_target_pairs={{1,113},{17,1},{33,17},{49,33},{65,49},{81,65},{97,81},{113,97},{1... | collective-permute-start | bytes 1572872 | tf_op jit(solution)/shard_map/ppermute | solution.py:26
  37.5 2.0 %collective-permute-done.below = bf16[2,8,128,128]{3,2,1,0:T(8,128)(2,1)S(1)} collective-permute-done((bf16[2,8,128,128]{3,2,1,0:T(8,128)(2,1)}, bf16[2,8,128,128]{3,2,1,0:T(8,128)(2,1)S(1)}, u32[]{:S(2)}, u32[]{:S(2)}) %collective-permute-start) | collective-permute-done | bytes 524320 | tf_op jit(solution)/shard_map/ppermute | solution.py:26
  39.5 4.9 %collective-permute-done.1.above = bf16[2,8,128,128]{3,2,1,0:T(8,128)(2,1)S(1)} collective-permute-done((bf16[2,8,128,128]{3,2,1,0:T(8,128)(2,1)}, bf16[2,8,128,128]{3,2,1,0:T(8,128)(2,1)S(1)}, u32[]{:S(2)}, u32[]{:S(2)}) %collective-permute-start.1) | collective-permute-done | bytes 524320 | tf_op jit(solution)/shard_map/ppermute | solution.py:26
  44.5 0.0 copy-start.1
  44.5 1.2 %copy-done.1 = bf16[4,8,128,128]{3,2,1,0:T(8,128)(2,1)S(1)} copy-done((bf16[4,8,128,128]{3,2,1,0:T(8,128)(2,1)S(1)}, bf16[4,8,128,128]{3,2,1,0:T(8,128)(2,1)}, u32[]{:S(2)}) %copy-start.1) | copy-done | bytes 1048600
  45.7 0.3 shard_map.61
  46.0 33.0 %all_to_all.15.blocks = bf16[4,16,128,128]{3,2,1,0:T(8,128)(2,1)S(1)} all-to-all(bf16[4,16,128,128]{3,2,1,0:T(8,128)(2,1)S(1)} %shard_map.61), channel_id=1, replica_groups={{1,33,65,97},{17,49,81,113},{129,161,193,225},{145,177,209,241},{257,28..., dimensions={0} | all-to-all | bytes 4194304 | tf_op jit(solution)/shard_map/all_to_all | solution.py:149
  79.1 1.1 %shard_map.62 = (bf16[8,128,128]{2,1,0:T(8,128)(2,1)S(1)}, bf16[2,8,128,128]{3,2,1,0:T(8,128)(2,1)}, bf16[2,8,128,128]{3,2,1,0:T(8,128)(2,1)}) custom-call(bf16[4,16,128,128]{3,2,1,0:T(8,128)(2,1)S(1)} %all_to_all.15.blocks), custom_call_target="tpu_custom_call" | custom-call | bytes 3407872 | tf_op jit(solution)/shard_map/pallas_call | solution.py:132
  80.2 0.0 copy-start.2
  80.2 0.7 copy-done.2
  80.9 2.5 %collective-permute-start.2 = (bf16[2,8,128,128]{3,2,1,0:T(8,128)(2,1)}, bf16[2,8,128,128]{3,2,1,0:T(8,128)(2,1)S(1)}, u32[]{:S(2)}, u32[]{:S(2)}) collective-permute-start(bf16[2,8,128,128]{3,2,1,0:T(8,128)(2,1)} %get-tuple-element.18), channel_id=1, source_target_pairs={{1,17},{17,33},{33,49},{49,65},{65,81},{81,97},{97,113},{113,1},{1... | collective-permute-start | bytes 1572872 | tf_op jit(solution)/shard_map/ppermute | solution.py:26
  83.4 4.6 %collective-permute-start.3 = (bf16[2,8,128,128]{3,2,1,0:T(8,128)(2,1)}, bf16[2,8,128,128]{3,2,1,0:T(8,128)(2,1)S(1)}, u32[]{:S(2)}, u32[]{:S(2)}) collective-permute-start(bf16[2,8,128,128]{3,2,1,0:T(8,128)(2,1)} %get-tuple-element.19), channel_id=1, source_target_pairs={{1,113},{17,1},{33,17},{49,33},{65,49},{81,65},{97,81},{113,97},{1... | collective-permute-start | bytes 1572872 | tf_op jit(solution)/shard_map/ppermute | solution.py:26
  88.0 5.7 %all-to-all-start.2 = ((bf16[8,128,128]{2,1,0:T(8,128)(2,1)}), bf16[8,128,128]{2,1,0:T(8,128)(2,1)S(1)}, u32[]{:S(2)}, u32[]{:S(2)}) async-start(bf16[8,128,128]{2,1,0:T(8,128)(2,1)} %copy-done.2), calls=%async_computation.2 | async-start | bytes 524288 | tf_op jit(solution)/shard_map/all_to_all | solution.py:149
  93.6 2.2 %collective-permute-done.2.below = bf16[2,8,128,128]{3,2,1,0:T(8,128)(2,1)S(1)} collective-permute-done((bf16[2,8,128,128]{3,2,1,0:T(8,128)(2,1)}, bf16[2,8,128,128]{3,2,1,0:T(8,128)(2,1)S(1)}, u32[]{:S(2)}, u32[]{:S(2)}) %collective-permute-start.2) | collective-permute-done | bytes 524320 | tf_op jit(solution)/shard_map/ppermute | solution.py:26
  95.9 1.6 %collective-permute-done.3.above = bf16[2,8,128,128]{3,2,1,0:T(8,128)(2,1)S(1)} collective-permute-done((bf16[2,8,128,128]{3,2,1,0:T(8,128)(2,1)}, bf16[2,8,128,128]{3,2,1,0:T(8,128)(2,1)S(1)}, u32[]{:S(2)}, u32[]{:S(2)}) %collective-permute-start.3) | collective-permute-done | bytes 524320 | tf_op jit(solution)/shard_map/ppermute | solution.py:26
  97.5 0.0 copy-start
  97.5 3.4 %copy-done = bf16[512,8192]{1,0:T(8,128)(2,1)S(1)} copy-done((bf16[512,8192]{1,0:T(8,128)(2,1)S(1)}, bf16[512,8192]{1,0:T(8,128)(2,1)}, u32[]{:S(2)}) %copy-start) | copy-done | bytes 8388632
  100.9 3.1 %shard_map.63 = bf16[512,128]{1,0:T(8,128)(2,1)} custom-call(bf16[512,8192]{1,0:T(8,128)(2,1)S(1)} %copy-done, bf16[4,16,128,128]{3,2,1,0:T(8,128)(2,1)S(1)} %all_to_all.15.blocks, bf16[2,8,128,128]{3,2,1,0:T(8,128)(2,1)S(1)} %collective-permute-done.2.below, bf16[2,8,128,128]{3,2,1,0:T(8,128)(2,1)S(1)} %collective-permute-done.3.above), custom_call_target="tpu_custom_call" | custom-call | flops 1073741824 | bytes 11665408 | tf_op jit(solution)/shard_map/pallas_call | solution.py:132
  104.0 0.1 all-to-all-done.2.blocks
  104.1 0.7 shard_map.64
Async XLA Ops:
  0.6 0.8 copy-start.3
  1.4 0.7 copy-start.4
  2.8 17.3 %all-to-all-start = ((bf16[8,128,128]{2,1,0:T(8,128)(2,1)}), bf16[8,128,128]{2,1,0:T(8,128)(2,1)S(1)}, u32[]{:S(2)}, u32[]{:S(2)}) async-start(bf16[8,128,128]{2,1,0:T(8,128)(2,1)} %shard_map.60), calls=%async_computation | async-start | bytes 524288 | tf_op jit(solution)/shard_map/all_to_all | solution.py:149
  14.8 24.7 %collective-permute-start = (bf16[2,8,128,128]{3,2,1,0:T(8,128)(2,1)}, bf16[2,8,128,128]{3,2,1,0:T(8,128)(2,1)S(1)}, u32[]{:S(2)}, u32[]{:S(2)}) collective-permute-start(bf16[2,8,128,128]{3,2,1,0:T(8,128)(2,1)} %get-tuple-element.13), channel_id=1, source_target_pairs={{1,17},{17,33},{33,49},{49,65},{65,81},{81,97},{97,113},{113,1},{1... | collective-permute-start | bytes 1572872 | tf_op jit(solution)/shard_map/ppermute | solution.py:26
  20.0 24.4 %collective-permute-start.1 = (bf16[2,8,128,128]{3,2,1,0:T(8,128)(2,1)}, bf16[2,8,128,128]{3,2,1,0:T(8,128)(2,1)S(1)}, u32[]{:S(2)}, u32[]{:S(2)}) collective-permute-start(bf16[2,8,128,128]{3,2,1,0:T(8,128)(2,1)} %get-tuple-element.15), channel_id=1, source_target_pairs={{1,113},{17,1},{33,17},{49,33},{65,49},{81,65},{97,81},{113,97},{1... | collective-permute-start | bytes 1572872 | tf_op jit(solution)/shard_map/ppermute | solution.py:26
  44.5 1.2 %copy-start.1 = (bf16[4,8,128,128]{3,2,1,0:T(8,128)(2,1)S(1)}, bf16[4,8,128,128]{3,2,1,0:T(8,128)(2,1)}, u32[]{:S(2)}) copy-start(bf16[4,8,128,128]{3,2,1,0:T(8,128)(2,1)} %get-tuple-element.12.keep) | copy-start | bytes 3145732
  80.2 0.7 copy-start.2
  80.9 14.9 %collective-permute-start.2 = (bf16[2,8,128,128]{3,2,1,0:T(8,128)(2,1)}, bf16[2,8,128,128]{3,2,1,0:T(8,128)(2,1)S(1)}, u32[]{:S(2)}, u32[]{:S(2)}) collective-permute-start(bf16[2,8,128,128]{3,2,1,0:T(8,128)(2,1)} %get-tuple-element.18), channel_id=1, source_target_pairs={{1,17},{17,33},{33,49},{49,65},{65,81},{81,97},{97,113},{113,1},{1... | collective-permute-start | bytes 1572872 | tf_op jit(solution)/shard_map/ppermute | solution.py:26
  83.4 14.1 %collective-permute-start.3 = (bf16[2,8,128,128]{3,2,1,0:T(8,128)(2,1)}, bf16[2,8,128,128]{3,2,1,0:T(8,128)(2,1)S(1)}, u32[]{:S(2)}, u32[]{:S(2)}) collective-permute-start(bf16[2,8,128,128]{3,2,1,0:T(8,128)(2,1)} %get-tuple-element.19), channel_id=1, source_target_pairs={{1,113},{17,1},{33,17},{49,33},{65,49},{81,65},{97,81},{113,97},{1... | collective-permute-start | bytes 1572872 | tf_op jit(solution)/shard_map/ppermute | solution.py:26
  88.0 16.1 %all-to-all-start.2 = ((bf16[8,128,128]{2,1,0:T(8,128)(2,1)}), bf16[8,128,128]{2,1,0:T(8,128)(2,1)S(1)}, u32[]{:S(2)}, u32[]{:S(2)}) async-start(bf16[8,128,128]{2,1,0:T(8,128)(2,1)} %copy-done.2), calls=%async_computation.2 | async-start | bytes 524288 | tf_op jit(solution)/shard_map/all_to_all | solution.py:149
  97.5 3.4 %copy-start = (bf16[512,8192]{1,0:T(8,128)(2,1)S(1)}, bf16[512,8192]{1,0:T(8,128)(2,1)}, u32[]{:S(2)}) copy-start(bf16[512,8192]{1,0:T(8,128)(2,1)} %act.3) | copy-start | bytes 25165828

commit v7 on v3

--- a/solution.py
+++ b/solution.py
@@ -1,5 +1,3 @@
-import functools
-
 import jax
 import jax.numpy as jnp
 from jax import lax
@@ -22,36 +20,46 @@
     return pltpu.CompilerParams(vmem_limit_bytes=mib * 1024 * 1024)
 
 
-def spot(first, outer, inner):
-    return jnp.where(first, inner, outer), jnp.where(first, outer, inner)
-
-
-def grad_kernel(act, cot, codes, scales, out, act_v, cot_v, codes_v, scales_v, sems):
+def grad_kernel(
+    act, cot, codes, scales, out, act_v, cot_v, codes_v, scales_v, out_v, weight_v, sems, out_sems
+):
     rows = codes.shape[0]
     chunk = act.shape[1] // SIDE
     part = lambda k: pl.ds(k * chunk, chunk)
+    blocks = pl.ds(0, SIDE)
     copies = [
-        pltpu.make_async_copy(cot, cot_v, sems.at[0]),
         pltpu.make_async_copy(codes, codes_v, sems.at[1]),
         pltpu.make_async_copy(scales, scales_v, sems.at[2]),
+        pltpu.make_async_copy(cot, cot_v, sems.at[0]),
     ] + [
         pltpu.make_async_copy(act.at[:, part(k)], act_v.at[k], sems.at[3 + k]) for k in range(SIDE)
     ]
     for copy in copies:
         copy.start()
     x_first = lax.axis_index("rep") == 0
+    copies[0].wait()
     copies[1].wait()
+    weight_v[...] = (codes_v[...].astype(jnp.float32) * scales_v[...]).astype(jnp.bfloat16)
+    sent = [
+        pltpu.make_async_copy(weight_v, out.at[peer, SIDE], out_sems.at[SIDE + peer])
+        for peer in range(SIDE)
+    ]
+    for copy in sent:
+        copy.start()
     copies[2].wait()
-    weight = (codes_v[...].astype(jnp.float32) * scales_v[...]).astype(jnp.bfloat16)
-    for peer in range(SIDE):
-        out[peer, SIDE] = weight
-    copies[0].wait()
     cot_t = cot_v[...].T
     for k in range(SIDE):
         copies[3 + k].wait()
         share = jnp.dot(cot_t, act_v[k], preferred_element_type=jnp.float32).astype(jnp.bfloat16)
         for j in range(SIDE):
-            out[spot(x_first, k, j)] = share[:, j * rows : (j + 1) * rows]
+            out_v[k, j] = share[:, j * rows : (j + 1) * rows]
+        across = pltpu.make_async_copy(out_v.at[k], out.at[blocks, k], out_sems.at[k])
+        along = pltpu.make_async_copy(out_v.at[k], out.at[k, blocks], out_sems.at[k])
+        pl.when(x_first)(across.start)
+        pl.when(jnp.logical_not(x_first))(along.start)
+        sent.append(along)
+    for copy in sent:
+        copy.wait()
 
 
 def middle_kernel(blocks, out):
@@ -67,15 +75,27 @@
 def keyvals_kernel(act, blocks, out, grad, weight):
     rows = blocks.shape[2]
     chunk = SIDE * rows
-    z_last = lax.axis_index("rep") == 1
-    total = None
-    for k in range(SIDE):
-        for j in range(SIDE):
-            weight[pl.ds((k * SIDE + j) * rows, rows)] = blocks[spot(z_last, k, j)]
-        part = pl.ds(k * chunk, chunk)
-        product = jnp.dot(act[:, part], weight[part], preferred_element_type=jnp.float32)
-        total = product if total is None else total + product
-    out[...] = total.astype(jnp.bfloat16)
+    part = lambda k: pl.ds(k * chunk, chunk)
+    z_last = lax.axis_index("rep") == 0
+
+    def multiply(weight_of):
+        total = None
+        for k in range(SIDE):
+            product = jnp.dot(act[:, part(k)], weight_of(k), preferred_element_type=jnp.float32)
+            total = product if total is None else total + product
+        out[...] = total.astype(jnp.bfloat16)
+
+    @pl.when(z_last)
+    def _():
+        multiply(lambda k: blocks[k, pl.ds(0, SIDE)].reshape(chunk, -1))
+
+    @pl.when(jnp.logical_not(z_last))
+    def _():
+        for k in range(SIDE):
+            for j in range(SIDE):
+                weight[pl.ds((k * SIDE + j) * rows, rows)] = blocks[j, k]
+        multiply(lambda k: weight[part(k)])
+
     share = blocks[0, SIDE].astype(jnp.float32)
     for peer in range(1, SIDE):
         share += blocks[peer, SIDE].astype(jnp.float32)
@@ -95,13 +115,16 @@
         grad_kernel,
         out_shape=jax.ShapeDtypeStruct(packed, jnp.bfloat16),
         in_specs=[hbm] * 4,
-        out_specs=vmem,
+        out_specs=hbm,
         scratch_shapes=[
             pltpu.VMEM((SIDE, tokens, width // SIDE), act.dtype),
             pltpu.VMEM(cotangent.shape, cotangent.dtype),
             pltpu.VMEM(codes.shape, codes.dtype),
             pltpu.VMEM(scales.shape, scales.dtype),
+            pltpu.VMEM((SIDE, SIDE, columns, rows), jnp.bfloat16),
+            pltpu.VMEM((rows, columns), jnp.bfloat16),
             pltpu.SemaphoreType.DMA((3 + SIDE,)),
+            pltpu.SemaphoreType.DMA((2 * SIDE,)),
         ],
         compiler_params=params(60),
         cost_estimate=cost,

time: 99.1 us -> 98.9 us (level)
  the two profiles are of different devices: /device:TPU:80 before, /device:TPU:32 now
where the time goes in v7:
time: 98.9 us; the launch traced here: 98.7 us
  blocking collectives  89.4 us (90%)
  Pallas kernels  8.65 us (9%)
    all_to_all x2, blocking collectives, body(): lax.all_to_all(blocks, AXES, 0, 0, axis_index_groups=groups)  89.4 us
    pallas_call x1, Pallas kernels, body(): pl.pallas_call(grad_kernel, out_shape=jax.ShapeDtypeStruct(packed, jnp.bf...  5.29 us
    pallas_call x1, Pallas kernels, body(): pl.pallas_call(keyvals_kernel, out_shape=(jax.ShapeDtypeStruct((tokens, c...  3.07 us

profile of v7, /device:TPU:32, one launch (start us, length us, event | category | flops | bytes accessed | tf_op | source)
XLA Modules:
  0.0 98.7 jit_solution(5614165904717071516)
XLA Ops:
  0.6 5.3 %shard_map.59 = bf16[8,9,128,128]{3,2,1,0:T(8,128)(2,1)} custom-call(bf16[512,8192]{1,0:T(8,128)(2,1)} %act.3, bf16[512,128]{1,0:T(8,128)(2,1)} %cot.1, bf16[128,128]{1,0:T(8,128)(2,1)} %codes.1, f32[1,128]{1,0:T(1,128)} %scales.1), custom_call_target="tpu_custom_call" | custom-call | flops 1073741824 | bytes 8388608 | tf_op jit(solution)/shard_map/pallas_call | solution.py:114
  5.9 39.7 %all_to_all.10.blocks = bf16[8,9,128,128]{3,2,1,0:T(8,128)(2,1)S(1)} all-to-all(bf16[8,9,128,128]{3,2,1,0:T(8,128)(2,1)} %shard_map.59), channel_id=1, replica_groups={{0,16,32,48,64,80,96,112},{128,144,160,176,192,208,224,240},{256,272,28..., dimensions={0} | all-to-all | bytes 4718592 | tf_op jit(solution)/shard_map/all_to_all | solution.py:112
  45.6 0.0 copy-start
  45.6 0.3 shard_map.60
  45.9 49.7 %all_to_all.11.blocks = bf16[8,9,128,128]{3,2,1,0:T(8,128)(2,1)S(1)} all-to-all(bf16[8,9,128,128]{3,2,1,0:T(8,128)(2,1)S(1)} %shard_map.60), channel_id=1, replica_groups={{1,17,33,49,65,81,97,113},{129,145,161,177,193,209,225,241},{257,273,28..., dimensions={0} | all-to-all | bytes 4718592 | tf_op jit(solution)/shard_map/all_to_all | solution.py:112
  95.6 0.0 copy-done
  95.6 3.1 %shard_map.61 = (bf16[512,128]{1,0:T(8,128)(2,1)}, f32[128,128]{1,0:T(8,128)}) custom-call(bf16[512,8192]{1,0:T(8,128)(2,1)S(1)} %copy-done, bf16[8,9,128,128]{3,2,1,0:T(8,128)(2,1)S(1)} %all_to_all.11.blocks), custom_call_target="tpu_custom_call" | custom-call | flops 1073741824 | bytes 8388608 | tf_op jit(solution)/shard_map/pallas_call | solution.py:142
Async XLA Ops:
  45.6 50.0 %copy-start = (bf16[512,8192]{1,0:T(8,128)(2,1)S(1)}, bf16[512,8192]{1,0:T(8,128)(2,1)}, u32[]{:S(2)}) copy-start(bf16[512,8192]{1,0:T(8,128)(2,1)} %act.3) | copy-start | bytes 25165828

commit v8 on v3

--- a/solution.py
+++ b/solution.py
@@ -1,5 +1,3 @@
-import functools
-
 import jax
 import jax.numpy as jnp
 from jax import lax
@@ -11,10 +9,14 @@
 AXES = ("z", "x", "rep")
 
 
+def listed(place):
+    return 3 * place % SIDE
+
+
 def lines(first):
     at = lambda z, x, r: (z * SIDE + x) * 2 + r
-    along_x = [[at(z, x, first) for x in range(SIDE)] for z in range(SIDE)]
-    along_z = [[at(z, x, 1 - first) for z in range(SIDE)] for x in range(SIDE)]
+    along_x = [[at(z, listed(x), first) for x in range(SIDE)] for z in range(SIDE)]
+    along_z = [[at(listed(z), x, 1 - first) for z in range(SIDE)] for x in range(SIDE)]
     return along_x + along_z
 
 
@@ -51,7 +53,7 @@
         copies[3 + k].wait()
         share = jnp.dot(cot_t, act_v[k], preferred_element_type=jnp.float32).astype(jnp.bfloat16)
         for j in range(SIDE):
-            out[spot(x_first, k, j)] = share[:, j * rows : (j + 1) * rows]
+            out[spot(x_first, listed(k), listed(j))] = share[:, j * rows : (j + 1) * rows]
 
 
 def middle_kernel(blocks, out):
@@ -71,7 +73,7 @@
     total = None
     for k in range(SIDE):
         for j in range(SIDE):
-            weight[pl.ds((k * SIDE + j) * rows, rows)] = blocks[spot(z_last, k, j)]
+            weight[pl.ds((k * SIDE + j) * rows, rows)] = blocks[spot(z_last, listed(k), listed(j))]
         part = pl.ds(k * chunk, chunk)
         product = jnp.dot(act[:, part], weight[part], preferred_element_type=jnp.float32)
         total = product if total is None else total + product

time: 99.1 us -> 97.7 us (0.986)
  blocking collectives: 89.4 us -> 88 us
    all_to_all x2, blocking collectives: 89.4 us -> 88 us  [body(): lax.all_to_all(blocks, AXES, 0, 0, axis_index_groups=groups)]
where the time goes in v8:
time: 97.7 us; the launch traced here: 97.5 us
  blocking collectives  88 us (90%)
  Pallas kernels  8.84 us (9%)
    all_to_all x2, blocking collectives, body(): lax.all_to_all(blocks, AXES, 0, 0, axis_index_groups=groups)  88 us
    pallas_call x1, Pallas kernels, body(): pl.pallas_call(grad_kernel, out_shape=jax.ShapeDtypeStruct(packed, jnp.bf...  5.37 us
    pallas_call x1, Pallas kernels, body(): pl.pallas_call(keyvals_kernel, out_shape=(jax.ShapeDtypeStruct((tokens, c...  3.19 us

profile of v8, /device:TPU:80, one launch (start us, length us, event | category | flops | bytes accessed | tf_op | source)
XLA Modules:
  0.0 97.5 jit_solution(11764040982385721631)
XLA Ops:
  0.6 5.4 %shard_map.59 = bf16[8,9,128,128]{3,2,1,0:T(8,128)(2,1)} custom-call(bf16[512,8192]{1,0:T(8,128)(2,1)} %act.3, bf16[512,128]{1,0:T(8,128)(2,1)} %cot.1, bf16[128,128]{1,0:T(8,128)(2,1)} %codes.1, f32[1,128]{1,0:T(1,128)} %scales.1), custom_call_target="tpu_custom_call" | custom-call | flops 1073741824 | bytes 8388608 | tf_op jit(solution)/shard_map/pallas_call | solution.py:96
  6.0 39.0 %all_to_all.10.blocks = bf16[8,9,128,128]{3,2,1,0:T(8,128)(2,1)S(1)} all-to-all(bf16[8,9,128,128]{3,2,1,0:T(8,128)(2,1)} %shard_map.59), channel_id=1, replica_groups={{0,48,96,16,64,112,32,80},{128,176,224,144,192,240,160,208},{256,304,35..., dimensions={0} | all-to-all | bytes 4718592 | tf_op jit(solution)/shard_map/all_to_all | solution.py:94
  45.0 0.0 copy-start
  45.0 0.3 shard_map.60
  45.3 49.0 %all_to_all.11.blocks = bf16[8,9,128,128]{3,2,1,0:T(8,128)(2,1)S(1)} all-to-all(bf16[8,9,128,128]{3,2,1,0:T(8,128)(2,1)S(1)} %shard_map.60), channel_id=1, replica_groups={{1,49,97,17,65,113,33,81},{129,177,225,145,193,241,161,209},{257,305,35..., dimensions={0} | all-to-all | bytes 4718592 | tf_op jit(solution)/shard_map/all_to_all | solution.py:94
  94.3 0.0 copy-done
  94.3 3.2 %shard_map.61 = (bf16[512,128]{1,0:T(8,128)(2,1)}, f32[128,128]{1,0:T(8,128)}) custom-call(bf16[512,8192]{1,0:T(8,128)(2,1)S(1)} %copy-done, bf16[8,9,128,128]{3,2,1,0:T(8,128)(2,1)S(1)} %all_to_all.11.blocks), custom_call_target="tpu_custom_call" | custom-call | flops 1073741824 | bytes 8388608 | tf_op jit(solution)/shard_map/pallas_call | solution.py:121
Async XLA Ops:
  45.0 49.3 %copy-start = (bf16[512,8192]{1,0:T(8,128)(2,1)S(1)}, bf16[512,8192]{1,0:T(8,128)(2,1)}, u32[]{:S(2)}) copy-start(bf16[512,8192]{1,0:T(8,128)(2,1)} %act.3) | copy-start | bytes 25165828

commit v9 on v8

--- a/solution.py
+++ b/solution.py
@@ -13,19 +13,15 @@
     return 3 * place % SIDE
 
 
-def lines(first):
+def lines(first, order):
     at = lambda z, x, r: (z * SIDE + x) * 2 + r
-    along_x = [[at(z, listed(x), first) for x in range(SIDE)] for z in range(SIDE)]
-    along_z = [[at(listed(z), x, 1 - first) for z in range(SIDE)] for x in range(SIDE)]
+    along_x = [[at(z, order(x), first) for x in range(SIDE)] for z in range(SIDE)]
+    along_z = [[at(order(z), x, 1 - first) for z in range(SIDE)] for x in range(SIDE)]
     return along_x + along_z
 
 
 def params(mib=32):
     return pltpu.CompilerParams(vmem_limit_bytes=mib * 1024 * 1024)
-
-
-def spot(first, outer, inner):
-    return jnp.where(first, inner, outer), jnp.where(first, outer, inner)
 
 
 def grad_kernel(act, cot, codes, scales, out, act_v, cot_v, codes_v, scales_v, sems):
@@ -53,7 +49,8 @@
         copies[3 + k].wait()
         share = jnp.dot(cot_t, act_v[k], preferred_element_type=jnp.float32).astype(jnp.bfloat16)
         for j in range(SIDE):
-            out[spot(x_first, listed(k), listed(j))] = share[:, j * rows : (j + 1) * rows]
+            peer, rest = jnp.where(x_first, listed(j), listed(k)), jnp.where(x_first, k, j)
+            out[peer, rest] = share[:, j * rows : (j + 1) * rows]
 
 
 def middle_kernel(blocks, out):
@@ -73,7 +70,8 @@
     total = None
     for k in range(SIDE):
         for j in range(SIDE):
-            weight[pl.ds((k * SIDE + j) * rows, rows)] = blocks[spot(z_last, listed(k), listed(j))]
+            peer, rest = jnp.where(z_last, j, k), jnp.where(z_last, listed(k), listed(j))
+            weight[pl.ds((k * SIDE + j) * rows, rows)] = blocks[peer, rest]
         part = pl.ds(k * chunk, chunk)
         product = jnp.dot(act[:, part], weight[part], preferred_element_type=jnp.float32)
         total = product if total is None else total + product
@@ -108,7 +106,7 @@
         compiler_params=params(60),
         cost_estimate=cost,
     )(act, cotangent, codes, scales)
-    arrived = exchange(sent, lines(0))
+    arrived = exchange(sent, lines(0, listed))
     sent = pl.pallas_call(
         middle_kernel,
         out_shape=jax.ShapeDtypeStruct(packed, jnp.bfloat16),
@@ -116,7 +114,7 @@
         out_specs=vmem,
         compiler_params=params(),
     )(arrived)
-    arrived = exchange(sent, lines(1))
+    arrived = exchange(sent, lines(1, int))
     return tuple(
         pl.pallas_call(
             keyvals_kernel,

time: 97.7 us -> 98.4 us (level)
  no operation moved by 1% of the time
where the time goes in v9:
time: 98.4 us; the launch traced here: 98.2 us
  blocking collectives  88.7 us (90%)
  Pallas kernels  8.84 us (9%)
    all_to_all x2, blocking collectives, body(): lax.all_to_all(blocks, AXES, 0, 0, axis_index_groups=groups)  88.7 us
    pallas_call x1, Pallas kernels, body(): pl.pallas_call(grad_kernel, out_shape=jax.ShapeDtypeStruct(packed, jnp.bf...  5.37 us
    pallas_call x1, Pallas kernels, body(): pl.pallas_call(keyvals_kernel, out_shape=(jax.ShapeDtypeStruct((tokens, c...  3.19 us

profile of v9, /device:TPU:80, one launch (start us, length us, event | category | flops | bytes accessed | tf_op | source)
XLA Modules:
  0.0 98.2 jit_solution(13543673171122570440)
XLA Ops:
  0.6 5.4 %shard_map.59 = bf16[8,9,128,128]{3,2,1,0:T(8,128)(2,1)} custom-call(bf16[512,8192]{1,0:T(8,128)(2,1)} %act.3, bf16[512,128]{1,0:T(8,128)(2,1)} %cot.1, bf16[128,128]{1,0:T(8,128)(2,1)} %codes.1, f32[1,128]{1,0:T(1,128)} %scales.1), custom_call_target="tpu_custom_call" | custom-call | flops 1073741824 | bytes 8388608 | tf_op jit(solution)/shard_map/pallas_call | solution.py:94
  6.0 39.0 %all_to_all.10.blocks = bf16[8,9,128,128]{3,2,1,0:T(8,128)(2,1)S(1)} all-to-all(bf16[8,9,128,128]{3,2,1,0:T(8,128)(2,1)} %shard_map.59), channel_id=1, replica_groups={{0,48,96,16,64,112,32,80},{128,176,224,144,192,240,160,208},{256,304,35..., dimensions={0} | all-to-all | bytes 4718592 | tf_op jit(solution)/shard_map/all_to_all | solution.py:92
  45.0 0.0 copy-start
  45.0 0.3 shard_map.60
  45.3 49.7 %all_to_all.11.blocks = bf16[8,9,128,128]{3,2,1,0:T(8,128)(2,1)S(1)} all-to-all(bf16[8,9,128,128]{3,2,1,0:T(8,128)(2,1)S(1)} %shard_map.60), channel_id=1, replica_groups={{1,17,33,49,65,81,97,113},{129,145,161,177,193,209,225,241},{257,273,28..., dimensions={0} | all-to-all | bytes 4718592 | tf_op jit(solution)/shard_map/all_to_all | solution.py:92
  95.0 0.0 copy-done
  95.0 3.2 %shard_map.61 = (bf16[512,128]{1,0:T(8,128)(2,1)}, f32[128,128]{1,0:T(8,128)}) custom-call(bf16[512,8192]{1,0:T(8,128)(2,1)S(1)} %copy-done, bf16[8,9,128,128]{3,2,1,0:T(8,128)(2,1)S(1)} %all_to_all.11.blocks), custom_call_target="tpu_custom_call" | custom-call | flops 1073741824 | bytes 8388608 | tf_op jit(solution)/shard_map/pallas_call | solution.py:119
Async XLA Ops:
  45.0 50.0 %copy-start = (bf16[512,8192]{1,0:T(8,128)(2,1)S(1)}, bf16[512,8192]{1,0:T(8,128)(2,1)}, u32[]{:S(2)}) copy-start(bf16[512,8192]{1,0:T(8,128)(2,1)} %act.3) | copy-start | bytes 25165828
